TPU v7x, 256 devices: a whole 4x4x8 slice. The times are simulated.
256 devices in a mesh: ctx: 32 (over z, x), tp: 8 (over y, core).
Axes of the slice: x: 4, y: 4, z: 8, core: 2. Of those that a mesh axis runs over, the one named last changes fastest.
Arguments:
- query_vectors: bfloat16 [32768, 2048], P('ctx', 'tp'), may hold values from -160 to 160
- key_vectors: bfloat16 [32768, 2048], P('ctx', 'tp'), may hold values from -4 to 4
- value_vectors: bfloat16 [32768, 2048], P('ctx', 'tp'), may hold values from -6 to 6
- selections: int32 [64, 8, 8], P(None, 'tp'), may hold values from 0 to 63, as said below
- out_weight: bfloat16 [2048, 4096], P('tp'), may hold values from -0.125 to 0.125
Outputs:
- mixed_out: bfloat16 [32768, 4096], P(('ctx', 'tp'))
Inputs may be any that keep to these rules, and one draw needn't show every extreme that they name: `selections`: entries below their query block's own index are distinct; an entry not below it selects nothing. An index of ctx holds 2 consecutive blocks; for each head group, the key blocks selected by the query blocks of one index lie on distinct indices, all below that index, so at most one key block of any index is selected by them.
All inputs are finite; a program needn't handle non-finite values.
Results may differ from a plain program's by a relative error of at most 0.019.
Values may be sent and summed in bfloat16 or wider, within the bound.
No kernel may reach another device: no remote copies, remote signals or barrier semaphores. Data moves between devices by JAX's collectives and lax.ppermute only.
A program may use at most 128 MiB of HBM per device.

v0:
```python
import math

import jax
import jax.numpy as jnp
from jax import lax
from jax.sharding import PartitionSpec as P

HD = 128
BLK = 512
GH = 2


NEG_FILL = -1e30


def block_terms(query_blk, key_blk, value_blk, visible, head_count):
    row_count = query_blk.shape[0]
    query_heads = query_blk.reshape(row_count, head_count, -1)
    key_heads = key_blk.reshape(key_blk.shape[0], head_count, -1)
    value_heads = value_blk.reshape(value_blk.shape[0], head_count, -1)
    scaling = 1.0 / math.sqrt(query_heads.shape[-1])
    scores = (
        jnp.einsum("qhd,khd->hqk", query_heads, key_heads, preferred_element_type=jnp.float32)
        * scaling
    )
    scores = jnp.where(visible, scores, NEG_FILL)
    maxima = jnp.max(scores, axis=-1)
    weights = jnp.where(visible, jnp.exp(scores - maxima[..., None]), 0.0)
    totals = jnp.sum(weights, axis=-1)
    summed = jnp.einsum(
        "hqk,khd->qhd",
        weights.astype(jnp.bfloat16),
        value_heads,
        preferred_element_type=jnp.float32,
    )
    return (summed.reshape(row_count, -1).astype(jnp.bfloat16), maxima, totals)


def empty_terms(row_count, feature_width, head_count):
    return (
        jnp.zeros((row_count, feature_width), jnp.bfloat16),
        jnp.full((head_count, row_count), NEG_FILL, jnp.float32),
        jnp.zeros((head_count, row_count), jnp.float32),
    )


def slot_table(hit_mask, chosen_blocks, local_blocks):
    usable = jnp.any(hit_mask, axis=(1, 3))
    rank_ids = jnp.arange(local_blocks, dtype=jnp.int32)[None, :, None, None]
    query_pos = jnp.sum(jnp.where(hit_mask, rank_ids, 0), axis=(1, 3))
    key_pos = jnp.sum(jnp.where(hit_mask, chosen_blocks % local_blocks, 0), axis=(1, 3))
    return (usable, query_pos, key_pos)


def key_side(selections, local_blocks, my_index):
    device_count = selections.shape[0] // local_blocks
    chosen_blocks = selections.reshape(
        device_count, local_blocks, selections.shape[1], selections.shape[2]
    )
    query_block = jnp.arange(device_count * local_blocks, dtype=jnp.int32).reshape(
        device_count, local_blocks, 1, 1
    )
    hit_mask = (chosen_blocks // local_blocks == my_index) & (chosen_blocks < query_block)
    return slot_table(hit_mask, chosen_blocks, local_blocks)


def query_side(selections, local_blocks, my_index):
    device_count = selections.shape[0] // local_blocks
    own_rows = lax.dynamic_slice_in_dim(selections, my_index * local_blocks, local_blocks, 0)
    query_block = my_index * local_blocks + jnp.arange(local_blocks, dtype=jnp.int32)[:, None, None]
    source_ids = jnp.arange(device_count, dtype=jnp.int32)[:, None, None, None]
    hit_mask = (own_rows[None] // local_blocks == source_ids) & (own_rows[None] < query_block[None])
    chosen_blocks = jnp.broadcast_to(own_rows[None], hit_mask.shape)
    return slot_table(hit_mask, chosen_blocks, local_blocks)


def pair_loop(query_fetch, key_fetch, value_fetch, usable, group_count, group_width):
    slot_count = usable.shape[0]

    def single_pair(pair_index):
        source_slot = pair_index // group_count
        group_pos = pair_index % group_count

        def compute_part():
            return block_terms(
                query_fetch(source_slot, group_pos),
                key_fetch(source_slot, group_pos),
                value_fetch(source_slot, group_pos),
                True,
                GH,
            )

        def skip_part():
            return empty_terms(BLK, group_width, GH)

        return lax.cond(usable[source_slot, group_pos], compute_part, skip_part)

    pair_sums, pair_max, pair_totals = lax.map(
        single_pair, jnp.arange(slot_count * group_count, dtype=jnp.int32)
    )
    return (
        pair_sums.reshape(slot_count, group_count, BLK, group_width),
        pair_max.reshape(slot_count, group_count, GH, BLK),
        pair_totals.reshape(slot_count, group_count, GH, BLK),
    )


def merge_parts(
    own_sums, own_max, own_totals, part_sums, part_max, part_totals, usable, query_pos, group_count
):
    local_blocks, row_count, feature_width = own_sums.shape
    slot_count = part_sums.shape[0]
    part_values = part_sums.reshape(slot_count, group_count, row_count, GH, HD)
    merged_rows = []
    for block_pos in range(local_blocks):
        chosen_mask = usable & (query_pos == block_pos)
        slot_max = jnp.where(chosen_mask[:, :, None, None], part_max, NEG_FILL)
        self_max = own_max[block_pos].reshape(group_count, GH, row_count)
        self_total = own_totals[block_pos].reshape(group_count, GH, row_count)
        self_sums = jnp.swapaxes(own_sums[block_pos].reshape(row_count, group_count, GH, HD), 0, 1)
        best_max = jnp.maximum(self_max, jnp.max(slot_max, axis=0))
        self_factor = jnp.exp(self_max - best_max)
        slot_factor = jnp.exp(slot_max - best_max[None])
        denominator = self_factor * self_total + jnp.sum(slot_factor * part_totals, axis=0)
        numerator = jnp.swapaxes(self_factor, 1, 2)[..., None] * self_sums.astype(jnp.float32)
        numerator = numerator + jnp.sum(
            jnp.swapaxes(slot_factor, 2, 3)[..., None] * part_values.astype(jnp.float32), axis=0
        )
        attention_block = numerator / jnp.swapaxes(denominator, 1, 2)[..., None]
        merged_rows.append(
            jnp.swapaxes(attention_block, 0, 1)
            .reshape(row_count, feature_width)
            .astype(jnp.bfloat16)
        )
    return jnp.concatenate(merged_rows, 0)


def local(query_vectors, key_vectors, value_vectors, selections, out_weight):
    tok_rows = query_vectors.shape[0]
    feature_width = query_vectors.shape[1]
    head_count = feature_width // HD
    group_count = head_count // GH
    group_width = GH * HD
    local_blocks = tok_rows // BLK
    my_index = lax.axis_index("ctx")
    causal = jnp.tril(jnp.ones((BLK, BLK), dtype=bool))[None]
    query_sets = query_vectors.reshape(local_blocks, BLK, feature_width)
    key_sets = key_vectors.reshape(local_blocks, BLK, feature_width)
    value_sets = value_vectors.reshape(local_blocks, BLK, feature_width)

    def own_block(query_one, key_one, value_one):
        return block_terms(query_one, key_one, value_one, causal, head_count)

    own_sums, own_max, own_totals = jax.vmap(own_block)(query_sets, key_sets, value_sets)
    query_grouped = query_vectors.reshape(local_blocks, BLK, group_count, group_width)
    key_grouped = key_vectors.reshape(local_blocks, BLK, group_count, group_width)
    value_grouped = value_vectors.reshape(local_blocks, BLK, group_count, group_width)
    group_ids = jnp.arange(group_count, dtype=jnp.int32)[None, :]
    own_usable, own_query, own_key = query_side(selections, local_blocks, my_index)
    their_usable, their_query, their_key = key_side(selections, local_blocks, my_index)
    sent_queries = query_grouped[own_query, :, group_ids]
    asked_rows = lax.all_to_all(sent_queries, "ctx", split_axis=0, concat_axis=0, tiled=True)

    def asked_query(source_slot, group_pos):
        return asked_rows[source_slot, group_pos]

    def local_key(source_slot, group_pos):
        return key_grouped[their_key[source_slot, group_pos], :, group_pos]

    def local_value(source_slot, group_pos):
        return value_grouped[their_key[source_slot, group_pos], :, group_pos]

    part_sums, part_max, part_totals = pair_loop(
        asked_query, local_key, local_value, their_usable, group_count, group_width
    )
    part_sums = lax.all_to_all(part_sums, "ctx", split_axis=0, concat_axis=0, tiled=True)
    part_max, part_totals = (
        lax.all_to_all(
            part_max.astype(jnp.bfloat16), "ctx", split_axis=0, concat_axis=0, tiled=True
        ).astype(part_max.dtype),
        lax.all_to_all(
            part_totals.astype(jnp.bfloat16), "ctx", split_axis=0, concat_axis=0, tiled=True
        ).astype(part_totals.dtype),
    )
    attention = merge_parts(
        own_sums,
        own_max,
        own_totals,
        part_sums,
        part_max,
        part_totals,
        own_usable,
        own_query,
        group_count,
    )
    return lax.psum_scatter(
        jnp.dot(attention, out_weight, preferred_element_type=jnp.float32).astype(jnp.bfloat16),
        "tp",
        scatter_dimension=0,
        tiled=True,
    )


def solution(mesh):
    in_specs = (P("ctx", "tp"), P("ctx", "tp"), P("ctx", "tp"), P(None, "tp", None), P("tp", None))
    out_specs = P(("ctx", "tp"), None)
    return jax.shard_map(local, mesh=mesh, in_specs=in_specs, out_specs=out_specs, check_vma=False)
```

profile of v0, /device:TPU:1, one launch (start us, length us, event | category | flops | bytes accessed | tf_op | source)
XLA Modules:
  0.0 1005.1 jit_solution(933418197510957045)
XLA Ops:
  13.5 12.3 %all-to-all-start = ((bf16[32,1,512,256]{3,2,1,0:T(8,128)(2,1)}), bf16[32,1,512,256]{3,2,1,0:T(8,128)(2,1)}, u32[]{:S(2)}, u32[]{:S(2)}) async-start(bf16[32,1,512,256]{3,2,1,0:T(8,128)(2,1)} %bitcast.122), calls=%async_computation | async-start | bytes 16777216 | tf_op jit(solution)/shard_map/all_to_all | solution.py:162
  29.0 184.4 %all-to-all-done = bf16[32,1,512,256]{3,2,1,0:T(8,128)(2,1)} async-done(((bf16[32,1,512,256]{3,2,1,0:T(8,128)(2,1)}), bf16[32,1,512,256]{3,2,1,0:T(8,128)(2,1)}, u32[]{:S(2)}, u32[]{:S(2)}) %all-to-all-start) | async-done | bytes 8388640 | tf_op jit(solution)/shard_map/all_to_all | solution.py:162
  213.3 12.0 %copy.53 = bf16[32,1,512,256]{2,3,1,0:T(8,128)(2,1)} copy(bf16[32,1,512,256]{3,2,1,0:T(8,128)(2,1)} %all-to-all-done) | data formatting | bytes 16777216 | tf_op jit(solution)/shard_map/while | solution.py:98
  225.8 473.8 %while.17 = (s32[]{:T(128)}, bf16[32,512,256]{1,2,0:T(8,128)(2,1)}, bf16[32,2,512]{2,1,0:T(2,128)(2,1)S(1)}, bf16[32,2,512]{2,1,0:T(2,128)(2,1)S(1)}, s32[32]{0:...) while((s32[]{:T(128)}, bf16[32,512,256]{1,2,0:T(8,128)(2,1)}, ...), condition=%wide.region_12.13_spmd, body=%wide.region_7.12_spmd.sunk | while | flops 272758784 | bytes 9464160 | solution.py:98
  237.6 10.2 %conditional.2 = (bf16[1,512,256]{1,2,0:T(8,128)(2,1)S(1)}, f32[1,2,512]{2,1,0:T(2,128)}, bf16[1,2,512]{2,1,0:T(2,128)(2,1)S(1)}) conditional(s32[]{:T(128)} %bitcast.118, () %tuple.70, (s32[]{:T(128)}, s32[32,1]{0,1:T(1,128)}, bf16[2,512,1,256]{1,3,2,0:T(8,128)(2,1)S(1)}, bf16[32,1,512,256]{2,3,1,0:T(8,128)(2,1)}, ...), branch_computations={%region_8.8_spmd, %region_9.11_spmd} | conditional | flops 272758784 | bytes 8927344 | solution.py:96
  253.8 10.2 %conditional.2 = (bf16[1,512,256]{1,2,0:T(8,128)(2,1)S(1)}, f32[1,2,512]{2,1,0:T(2,128)}, bf16[1,2,512]{2,1,0:T(2,128)(2,1)S(1)}) conditional(s32[]{:T(128)} %bitcast.118, () %tuple.70, (s32[]{:T(128)}, s32[32,1]{0,1:T(1,128)}, bf16[2,512,1,256]{1,3,2,0:T(8,128)(2,1)S(1)}, bf16[32,1,512,256]{2,3,1,0:T(8,128)(2,1)}, ...), branch_computations={%region_8.8_spmd, %region_9.11_spmd} | conditional | flops 272758784 | bytes 8927344 | solution.py:96
  270.0 10.2 %conditional.2 = (bf16[1,512,256]{1,2,0:T(8,128)(2,1)S(1)}, f32[1,2,512]{2,1,0:T(2,128)}, bf16[1,2,512]{2,1,0:T(2,128)(2,1)S(1)}) conditional(s32[]{:T(128)} %bitcast.118, () %tuple.70, (s32[]{:T(128)}, s32[32,1]{0,1:T(1,128)}, bf16[2,512,1,256]{1,3,2,0:T(8,128)(2,1)S(1)}, bf16[32,1,512,256]{2,3,1,0:T(8,128)(2,1)}, ...), branch_computations={%region_8.8_spmd, %region_9.11_spmd} | conditional | flops 272758784 | bytes 8927344 | solution.py:96
  286.3 10.2 %conditional.2 = (bf16[1,512,256]{1,2,0:T(8,128)(2,1)S(1)}, f32[1,2,512]{2,1,0:T(2,128)}, bf16[1,2,512]{2,1,0:T(2,128)(2,1)S(1)}) conditional(s32[]{:T(128)} %bitcast.118, () %tuple.70, (s32[]{:T(128)}, s32[32,1]{0,1:T(1,128)}, bf16[2,512,1,256]{1,3,2,0:T(8,128)(2,1)S(1)}, bf16[32,1,512,256]{2,3,1,0:T(8,128)(2,1)}, ...), branch_computations={%region_8.8_spmd, %region_9.11_spmd} | conditional | flops 272758784 | bytes 8927344 | solution.py:96
  302.5 10.2 %conditional.2 = (bf16[1,512,256]{1,2,0:T(8,128)(2,1)S(1)}, f32[1,2,512]{2,1,0:T(2,128)}, bf16[1,2,512]{2,1,0:T(2,128)(2,1)S(1)}) conditional(s32[]{:T(128)} %bitcast.118, () %tuple.70, (s32[]{:T(128)}, s32[32,1]{0,1:T(1,128)}, bf16[2,512,1,256]{1,3,2,0:T(8,128)(2,1)S(1)}, bf16[32,1,512,256]{2,3,1,0:T(8,128)(2,1)}, ...), branch_computations={%region_8.8_spmd, %region_9.11_spmd} | conditional | flops 272758784 | bytes 8927344 | solution.py:96
  318.7 10.2 %conditional.2 = (bf16[1,512,256]{1,2,0:T(8,128)(2,1)S(1)}, f32[1,2,512]{2,1,0:T(2,128)}, bf16[1,2,512]{2,1,0:T(2,128)(2,1)S(1)}) conditional(s32[]{:T(128)} %bitcast.118, () %tuple.70, (s32[]{:T(128)}, s32[32,1]{0,1:T(1,128)}, bf16[2,512,1,256]{1,3,2,0:T(8,128)(2,1)S(1)}, bf16[32,1,512,256]{2,3,1,0:T(8,128)(2,1)}, ...), branch_computations={%region_8.8_spmd, %region_9.11_spmd} | conditional | flops 272758784 | bytes 8927344 | solution.py:96
  334.9 10.2 %conditional.2 = (bf16[1,512,256]{1,2,0:T(8,128)(2,1)S(1)}, f32[1,2,512]{2,1,0:T(2,128)}, bf16[1,2,512]{2,1,0:T(2,128)(2,1)S(1)}) conditional(s32[]{:T(128)} %bitcast.118, () %tuple.70, (s32[]{:T(128)}, s32[32,1]{0,1:T(1,128)}, bf16[2,512,1,256]{1,3,2,0:T(8,128)(2,1)S(1)}, bf16[32,1,512,256]{2,3,1,0:T(8,128)(2,1)}, ...), branch_computations={%region_8.8_spmd, %region_9.11_spmd} | conditional | flops 272758784 | bytes 8927344 | solution.py:96
  351.1 10.2 %conditional.2 = (bf16[1,512,256]{1,2,0:T(8,128)(2,1)S(1)}, f32[1,2,512]{2,1,0:T(2,128)}, bf16[1,2,512]{2,1,0:T(2,128)(2,1)S(1)}) conditional(s32[]{:T(128)} %bitcast.118, () %tuple.70, (s32[]{:T(128)}, s32[32,1]{0,1:T(1,128)}, bf16[2,512,1,256]{1,3,2,0:T(8,128)(2,1)S(1)}, bf16[32,1,512,256]{2,3,1,0:T(8,128)(2,1)}, ...), branch_computations={%region_8.8_spmd, %region_9.11_spmd} | conditional | flops 272758784 | bytes 8927344 | solution.py:96
  383.5 10.2 %conditional.2 = (bf16[1,512,256]{1,2,0:T(8,128)(2,1)S(1)}, f32[1,2,512]{2,1,0:T(2,128)}, bf16[1,2,512]{2,1,0:T(2,128)(2,1)S(1)}) conditional(s32[]{:T(128)} %bitcast.118, () %tuple.70, (s32[]{:T(128)}, s32[32,1]{0,1:T(1,128)}, bf16[2,512,1,256]{1,3,2,0:T(8,128)(2,1)S(1)}, bf16[32,1,512,256]{2,3,1,0:T(8,128)(2,1)}, ...), branch_computations={%region_8.8_spmd, %region_9.11_spmd} | conditional | flops 272758784 | bytes 8927344 | solution.py:96
  399.7 10.2 %conditional.2 = (bf16[1,512,256]{1,2,0:T(8,128)(2,1)S(1)}, f32[1,2,512]{2,1,0:T(2,128)}, bf16[1,2,512]{2,1,0:T(2,128)(2,1)S(1)}) conditional(s32[]{:T(128)} %bitcast.118, () %tuple.70, (s32[]{:T(128)}, s32[32,1]{0,1:T(1,128)}, bf16[2,512,1,256]{1,3,2,0:T(8,128)(2,1)S(1)}, bf16[32,1,512,256]{2,3,1,0:T(8,128)(2,1)}, ...), branch_computations={%region_8.8_spmd, %region_9.11_spmd} | conditional | flops 272758784 | bytes 8927344 | solution.py:96
  415.9 10.2 %conditional.2 = (bf16[1,512,256]{1,2,0:T(8,128)(2,1)S(1)}, f32[1,2,512]{2,1,0:T(2,128)}, bf16[1,2,512]{2,1,0:T(2,128)(2,1)S(1)}) conditional(s32[]{:T(128)} %bitcast.118, () %tuple.70, (s32[]{:T(128)}, s32[32,1]{0,1:T(1,128)}, bf16[2,512,1,256]{1,3,2,0:T(8,128)(2,1)S(1)}, bf16[32,1,512,256]{2,3,1,0:T(8,128)(2,1)}, ...), branch_computations={%region_8.8_spmd, %region_9.11_spmd} | conditional | flops 272758784 | bytes 8927344 | solution.py:96
  432.1 10.2 %conditional.2 = (bf16[1,512,256]{1,2,0:T(8,128)(2,1)S(1)}, f32[1,2,512]{2,1,0:T(2,128)}, bf16[1,2,512]{2,1,0:T(2,128)(2,1)S(1)}) conditional(s32[]{:T(128)} %bitcast.118, () %tuple.70, (s32[]{:T(128)}, s32[32,1]{0,1:T(1,128)}, bf16[2,512,1,256]{1,3,2,0:T(8,128)(2,1)S(1)}, bf16[32,1,512,256]{2,3,1,0:T(8,128)(2,1)}, ...), branch_computations={%region_8.8_spmd, %region_9.11_spmd} | conditional | flops 272758784 | bytes 8927344 | solution.py:96
  448.3 10.2 %conditional.2 = (bf16[1,512,256]{1,2,0:T(8,128)(2,1)S(1)}, f32[1,2,512]{2,1,0:T(2,128)}, bf16[1,2,512]{2,1,0:T(2,128)(2,1)S(1)}) conditional(s32[]{:T(128)} %bitcast.118, () %tuple.70, (s32[]{:T(128)}, s32[32,1]{0,1:T(1,128)}, bf16[2,512,1,256]{1,3,2,0:T(8,128)(2,1)S(1)}, bf16[32,1,512,256]{2,3,1,0:T(8,128)(2,1)}, ...), branch_computations={%region_8.8_spmd, %region_9.11_spmd} | conditional | flops 272758784 | bytes 8927344 | solution.py:96
  464.5 10.2 %conditional.2 = (bf16[1,512,256]{1,2,0:T(8,128)(2,1)S(1)}, f32[1,2,512]{2,1,0:T(2,128)}, bf16[1,2,512]{2,1,0:T(2,128)(2,1)S(1)}) conditional(s32[]{:T(128)} %bitcast.118, () %tuple.70, (s32[]{:T(128)}, s32[32,1]{0,1:T(1,128)}, bf16[2,512,1,256]{1,3,2,0:T(8,128)(2,1)S(1)}, bf16[32,1,512,256]{2,3,1,0:T(8,128)(2,1)}, ...), branch_computations={%region_8.8_spmd, %region_9.11_spmd} | conditional | flops 272758784 | bytes 8927344 | solution.py:96
  480.7 10.2 %conditional.2 = (bf16[1,512,256]{1,2,0:T(8,128)(2,1)S(1)}, f32[1,2,512]{2,1,0:T(2,128)}, bf16[1,2,512]{2,1,0:T(2,128)(2,1)S(1)}) conditional(s32[]{:T(128)} %bitcast.118, () %tuple.70, (s32[]{:T(128)}, s32[32,1]{0,1:T(1,128)}, bf16[2,512,1,256]{1,3,2,0:T(8,128)(2,1)S(1)}, bf16[32,1,512,256]{2,3,1,0:T(8,128)(2,1)}, ...), branch_computations={%region_8.8_spmd, %region_9.11_spmd} | conditional | flops 272758784 | bytes 8927344 | solution.py:96
  496.9 10.2 %conditional.2 = (bf16[1,512,256]{1,2,0:T(8,128)(2,1)S(1)}, f32[1,2,512]{2,1,0:T(2,128)}, bf16[1,2,512]{2,1,0:T(2,128)(2,1)S(1)}) conditional(s32[]{:T(128)} %bitcast.118, () %tuple.70, (s32[]{:T(128)}, s32[32,1]{0,1:T(1,128)}, bf16[2,512,1,256]{1,3,2,0:T(8,128)(2,1)S(1)}, bf16[32,1,512,256]{2,3,1,0:T(8,128)(2,1)}, ...), branch_computations={%region_8.8_spmd, %region_9.11_spmd} | conditional | flops 272758784 | bytes 8927344 | solution.py:96
  520.4 10.2 %conditional.2 = (bf16[1,512,256]{1,2,0:T(8,128)(2,1)S(1)}, f32[1,2,512]{2,1,0:T(2,128)}, bf16[1,2,512]{2,1,0:T(2,128)(2,1)S(1)}) conditional(s32[]{:T(128)} %bitcast.118, () %tuple.70, (s32[]{:T(128)}, s32[32,1]{0,1:T(1,128)}, bf16[2,512,1,256]{1,3,2,0:T(8,128)(2,1)S(1)}, bf16[32,1,512,256]{2,3,1,0:T(8,128)(2,1)}, ...), branch_computations={%region_8.8_spmd, %region_9.11_spmd} | conditional | flops 272758784 | bytes 8927344 | solution.py:96
  543.8 10.2 %conditional.2 = (bf16[1,512,256]{1,2,0:T(8,128)(2,1)S(1)}, f32[1,2,512]{2,1,0:T(2,128)}, bf16[1,2,512]{2,1,0:T(2,128)(2,1)S(1)}) conditional(s32[]{:T(128)} %bitcast.118, () %tuple.70, (s32[]{:T(128)}, s32[32,1]{0,1:T(1,128)}, bf16[2,512,1,256]{1,3,2,0:T(8,128)(2,1)S(1)}, bf16[32,1,512,256]{2,3,1,0:T(8,128)(2,1)}, ...), branch_computations={%region_8.8_spmd, %region_9.11_spmd} | conditional | flops 272758784 | bytes 8927344 | solution.py:96
  583.5 10.2 %conditional.2 = (bf16[1,512,256]{1,2,0:T(8,128)(2,1)S(1)}, f32[1,2,512]{2,1,0:T(2,128)}, bf16[1,2,512]{2,1,0:T(2,128)(2,1)S(1)}) conditional(s32[]{:T(128)} %bitcast.118, () %tuple.70, (s32[]{:T(128)}, s32[32,1]{0,1:T(1,128)}, bf16[2,512,1,256]{1,3,2,0:T(8,128)(2,1)S(1)}, bf16[32,1,512,256]{2,3,1,0:T(8,128)(2,1)}, ...), branch_computations={%region_8.8_spmd, %region_9.11_spmd} | conditional | flops 272758784 | bytes 8927344 | solution.py:96
  615.9 10.2 %conditional.2 = (bf16[1,512,256]{1,2,0:T(8,128)(2,1)S(1)}, f32[1,2,512]{2,1,0:T(2,128)}, bf16[1,2,512]{2,1,0:T(2,128)(2,1)S(1)}) conditional(s32[]{:T(128)} %bitcast.118, () %tuple.70, (s32[]{:T(128)}, s32[32,1]{0,1:T(1,128)}, bf16[2,512,1,256]{1,3,2,0:T(8,128)(2,1)S(1)}, bf16[32,1,512,256]{2,3,1,0:T(8,128)(2,1)}, ...), branch_computations={%region_8.8_spmd, %region_9.11_spmd} | conditional | flops 272758784 | bytes 8927344 | solution.py:96
  632.1 10.2 %conditional.2 = (bf16[1,512,256]{1,2,0:T(8,128)(2,1)S(1)}, f32[1,2,512]{2,1,0:T(2,128)}, bf16[1,2,512]{2,1,0:T(2,128)(2,1)S(1)}) conditional(s32[]{:T(128)} %bitcast.118, () %tuple.70, (s32[]{:T(128)}, s32[32,1]{0,1:T(1,128)}, bf16[2,512,1,256]{1,3,2,0:T(8,128)(2,1)S(1)}, bf16[32,1,512,256]{2,3,1,0:T(8,128)(2,1)}, ...), branch_computations={%region_8.8_spmd, %region_9.11_spmd} | conditional | flops 272758784 | bytes 8927344 | solution.py:96
  655.5 10.2 %conditional.2 = (bf16[1,512,256]{1,2,0:T(8,128)(2,1)S(1)}, f32[1,2,512]{2,1,0:T(2,128)}, bf16[1,2,512]{2,1,0:T(2,128)(2,1)S(1)}) conditional(s32[]{:T(128)} %bitcast.118, () %tuple.70, (s32[]{:T(128)}, s32[32,1]{0,1:T(1,128)}, bf16[2,512,1,256]{1,3,2,0:T(8,128)(2,1)S(1)}, bf16[32,1,512,256]{2,3,1,0:T(8,128)(2,1)}, ...), branch_computations={%region_8.8_spmd, %region_9.11_spmd} | conditional | flops 272758784 | bytes 8927344 | solution.py:96
  687.9 10.2 %conditional.2 = (bf16[1,512,256]{1,2,0:T(8,128)(2,1)S(1)}, f32[1,2,512]{2,1,0:T(2,128)}, bf16[1,2,512]{2,1,0:T(2,128)(2,1)S(1)}) conditional(s32[]{:T(128)} %bitcast.118, () %tuple.70, (s32[]{:T(128)}, s32[32,1]{0,1:T(1,128)}, bf16[2,512,1,256]{1,3,2,0:T(8,128)(2,1)S(1)}, bf16[32,1,512,256]{2,3,1,0:T(8,128)(2,1)}, ...), branch_computations={%region_8.8_spmd, %region_9.11_spmd} | conditional | flops 272758784 | bytes 8927344 | solution.py:96
  699.6 11.8 %all_to_all.20 = bf16[32,1,2,512]{3,2,1,0:T(2,128)(2,1)S(1)} all-to-all(bf16[32,1,2,512]{3,2,1,0:T(2,128)(2,1)S(1)} %bitcast.131), channel_id=1, replica_groups=mesh['ctx'=32,'tp'=8] {'ctx'}, dimensions={0} | all-to-all | bytes 131072 | tf_op jit(solution)/shard_map/all_to_all | solution.py:181
  711.4 11.8 %all_to_all.21 = bf16[32,1,2,512]{3,2,1,0:T(2,128)(2,1)S(1)} all-to-all(bf16[32,1,2,512]{3,2,1,0:T(2,128)(2,1)S(1)} %bitcast.132), channel_id=1, replica_groups=mesh['ctx'=32,'tp'=8] {'ctx'}, dimensions={0} | all-to-all | bytes 131072 | tf_op jit(solution)/shard_map/all_to_all | solution.py:178
  737.0 176.3 %all-to-all-done.2 = bf16[32,1,512,256]{2,3,1,0:T(8,128)(2,1)} async-done(((bf16[32,1,512,256]{2,3,1,0:T(8,128)(2,1)}), bf16[32,1,512,256]{2,3,1,0:T(8,128)(2,1)}, u32[]{:S(2)}, u32[]{:S(2)}) %all-to-all-start.2) | async-done | bytes 8388640 | tf_op jit(solution)/shard_map/all_to_all | solution.py:176
  923.3 10.4 %fusion.6 = (f32[512,256]{0,1:T(8,128)S(1)}, f32[512,256]{0,1:T(8,128)S(1)}) fusion(f32[32,1,512,256]{2,3,1,0:T(8,128)} %bitcast.121, bf16[32,1,512,256]{2,3,1,0:T(8,128)(2,1)} %all-to-all-done.2, f32[32,1,512,256]{2,3,1,0:T(8,128)S(1)} %bitcast.120), kind=kLoop, calls=%fused_computation.19 | loop fusion | flops 20709376 | bytes 42991616 | tf_op jit(solution)/shard_map/reduce_sum | solution.py:126
  939.5 58.7 %reduce-scatter.2.cloned.1.call-done = bf16[128,4096]{1,0:T(8,128)(2,1)} async-done(((bf16[1024,4096]{1,0:T(8,128)(2,1)}), bf16[128,4096]{1,0:T(8,128)(2,1)}) %reduce-scatter.2.cloned.1.call-update) | async-done | bytes 1048592 | tf_op jit(solution)/shard_map/reduce_scatter | solution.py:196
  (401 shorter events, 365.9 us)
Async XLA Ops:
  6.5 927.4 %copy-start = (bf16[256,4096]{1,0:T(8,128)(2,1)S(1)}, bf16[256,4096]{1,0:T(8,128)(2,1)}, u32[]{:S(2)}) copy-start(bf16[256,4096]{1,0:T(8,128)(2,1)} %param.13) | copy-start | bytes 6291460
  13.5 12.4 %copy-start.4 = (s32[64,1,8]{0,2,1:T(8,128)S(1)}, s32[64,1,8]{0,2,1:T(8,128)}, u32[]{:S(2)}) copy-start(s32[64,1,8]{0,2,1:T(8,128)} %param.12) | copy-start | bytes 6148
  13.5 14.0 %copy-start.3 = (bf16[1024,256]{1,0:T(8,128)(2,1)S(1)}, bf16[1024,256]{1,0:T(8,128)(2,1)}, u32[]{:S(2)}) copy-start(bf16[1024,256]{1,0:T(8,128)(2,1)} %param.11) | copy-start | bytes 1572868
  13.5 199.8 %all-to-all-start = ((bf16[32,1,512,256]{3,2,1,0:T(8,128)(2,1)}), bf16[32,1,512,256]{3,2,1,0:T(8,128)(2,1)}, u32[]{:S(2)}, u32[]{:S(2)}) async-start(bf16[32,1,512,256]{3,2,1,0:T(8,128)(2,1)} %bitcast.122), calls=%async_computation | async-start | bytes 16777216 | tf_op jit(solution)/shard_map/all_to_all | solution.py:162
  723.2 5.3 copy-start.1
  723.2 6.3 copy-start.2
  723.2 190.0 %all-to-all-start.2 = ((bf16[32,1,512,256]{2,3,1,0:T(8,128)(2,1)}), bf16[32,1,512,256]{2,3,1,0:T(8,128)(2,1)}, u32[]{:S(2)}, u32[]{:S(2)}) async-start(bf16[32,1,512,256]{2,3,1,0:T(8,128)(2,1)} %bitcast.127), calls=%async_computation.2 | async-start | bytes 16777216 | tf_op jit(solution)/shard_map/all_to_all | solution.py:176
  728.3 269.9 %reduce-scatter.2.cloned.1.call-start = ((), (), s32[]{:S(2)}) async-start(), calls=%async_computation.5 | async-start | bytes 9437184 | tf_op jit(solution)/shard_map/reduce_scatter | solution.py:196
Sparse Core Ops, SparseCore 0:
  939.7 58.5 reduce-scatter.1
where the time goes:
time: 1010 us
  waiting for transfers between devices  419 us (41%)
  loops' own time  195 us (19%)
  local copies, waits for them, and re-layouts  183 us (18%)
  other arithmetic  81.6 us (8%)
  matrix products  71.5 us (7%)
  blocking collectives  23.7 us (2%)
  starting transfers between devices  17.6 us (2%)
  between operations  13.6 us (1%)
    all_to_all x1, waiting for transfers between devices, local(): lax.all_to_all(sent_queries, 'ctx', split_axis=0, concat_axis=0, tiled=True)  184 us
    all_to_all x1, waiting for transfers between devices, local(): lax.all_to_all(part_sums, 'ctx', split_axis=0, concat_axis=0, tiled=True)  176 us
    another operation x32, loops' own time, single_pair(): return lax.cond(usable[source_slot, group_pos], compute_part, skip_part)  129 us
    another operation x1, loops' own time, pair_loop(): lax.map(single_pair, jnp.arange(slot_count * group_count, dtype=jnp.int32))  66.3 us
    reduce_scatter x1, waiting for transfers between devices, local(): lax.psum_scatter(jnp.dot(attention, out_weight, preferred_element_type=jn...  58.7 us
    dynamic_update_slice x96, local copies, waits for them, and re-layouts, pair_loop(): lax.map(single_pair, jnp.arange(slot_count * group_count, dtype=jnp.int32))  45.9 us
    dynamic_slice x32, local copies, waits for them, and re-layouts, pair_loop(): lax.map(single_pair, jnp.arange(slot_count * group_count, dtype=jnp.int32))  40.3 us
    convert_element_type x32, other arithmetic, single_pair(): return lax.cond(usable[source_slot, group_pos], compute_part, skip_part)  39.2 us
  transfers between devices with their start and end apart: 3, of which 3 were waited for; matrix products, arithmetic and copies ran while one was open for 1% of the time, Pallas kernels for 0%

commit v1 on v0

v1 whole, which is shorter than its diff:
```python
import functools
import math

import jax
import jax.numpy as jnp
from jax import lax
from jax.experimental import pallas as pl
from jax.experimental.pallas import tpu as pltpu
from jax.sharding import Mesh, PartitionSpec as P

HD = 128
BLK = 512
SEL = 8
GH = 2
NZ, NX, NY, NC = 8, 4, 4, 2
N_TP = NY * NC
LOCAL = 2
ROWS = LOCAL * BLK // N_TP
STAT = 16
MSG = GH * HD + STAT
D = 4096
NEG = -1e30
SCALE = math.log2(math.e) / math.sqrt(HD)
F32 = jnp.float32
BF16 = jnp.bfloat16


def dot(a, b, dims):
    return lax.dot_general(a, b, (dims, ((), ())), preferred_element_type=F32)


def attend_kernel(pos_ref, sel_ref, q_ref, k_ref, vt_ref, out_ref, acc, top, tot):
    my_z = pos_ref[0]
    my_x = pos_ref[1]

    def step(slot, query, diagonal):
        row0 = pl.multiple_of(slot * BLK, BLK)
        for head in range(GH):
            cols = pl.ds(head * HD, HD)
            scores = dot(k_ref[pl.ds(row0, BLK), cols], query[:, head * HD : (head + 1) * HD], ((1,), (1,)))
            scores = scores * SCALE
            if diagonal:
                key_at = lax.broadcasted_iota(jnp.int32, (BLK, BLK), 0)
                query_at = lax.broadcasted_iota(jnp.int32, (BLK, BLK), 1)
                scores = jnp.where(key_at <= query_at, scores, NEG)
            old = top[head]
            new = jnp.maximum(old, jnp.max(scores, axis=0, keepdims=True))
            fade = jnp.exp2(old - new)
            weights = jnp.exp2(scores - new)
            top[head] = new
            tot[head] = tot[head] * fade + jnp.sum(weights, axis=0, keepdims=True)
            z_at = slot // LOCAL
            vt = vt_ref[z_at, pl.ds(head * HD, HD), pl.ds(pl.multiple_of(slot % LOCAL * BLK, BLK), BLK)]
            acc[head] = acc[head] * fade + dot(vt, weights.astype(BF16), ((1,), (0,)))

    def query_block(index, carry):
        x_at = index // LOCAL
        half = index % LOCAL
        block = (my_z * NX + x_at) * LOCAL + half
        acc[...] = jnp.zeros_like(acc)
        top[...] = jnp.full_like(top, NEG)
        tot[...] = jnp.zeros_like(tot)
        query = q_ref[pl.ds(pl.multiple_of(index * BLK, BLK), BLK), :]

        @pl.when(x_at == my_x)
        def _():
            step(my_z * LOCAL + half, query, True)

        def pick(at, c):
            key = sel_ref[block * SEL + at]
            owner = key // LOCAL

            @pl.when((key < block) & (owner % NX == my_x))
            def _():
                step(owner // NX * LOCAL + key % LOCAL, query, False)

            return c

        lax.fori_loop(0, SEL, pick, 0)
        pieces = BLK // ROWS
        for head in range(GH):
            total = tot[head]
            some = total > 0.0
            safe = jnp.where(some, total, 1.0)
            mean = (acc[head] / safe).astype(BF16)
            log_total = jnp.where(some, top[head] + jnp.log2(safe), NEG)
            high = log_total.astype(BF16)
            rest = log_total - high.astype(F32)
            mid = rest.astype(BF16)
            low = (rest - mid.astype(F32)).astype(BF16)
            for piece in range(pieces):
                lanes = slice(piece * ROWS, (piece + 1) * ROWS)
                at = x_at * N_TP + half * pieces + piece
                out_ref[at, pl.ds(head * HD, HD), :] = mean[:, lanes]
                stats = jnp.concatenate(
                    [
                        jnp.broadcast_to(part[:, lanes].astype(F32), (8, ROWS))
                        for part in (high, mid, low)
                    ],
                    axis=0,
                )
                row = lax.broadcasted_iota(jnp.int32, (8, ROWS), 0)
                packed = jnp.where(row == 0, stats[0:8], jnp.where(row == 1, stats[8:16], stats[16:24]))
                if head == 0:
                    firsts = [packed] if piece == 0 else firsts + [packed]
                else:
                    both = jnp.concatenate([firsts[piece], packed], axis=0).astype(BF16)
                    out_ref[at, pl.ds(GH * HD, STAT), :] = both
        return carry

    lax.fori_loop(0, NX * LOCAL, query_block, 0)


def attend(pos, sel, query, key, value_t):
    vmem = pl.BlockSpec(memory_space=pltpu.VMEM)
    smem = pl.BlockSpec(memory_space=pltpu.SMEM)
    return pl.pallas_call(
        attend_kernel,
        out_shape=jax.ShapeDtypeStruct((NX * N_TP, MSG, ROWS), BF16),
        in_specs=[smem, smem, vmem, vmem, vmem],
        out_specs=vmem,
        scratch_shapes=[
            pltpu.VMEM((GH, HD, BLK), F32),
            pltpu.VMEM((GH, 1, BLK), F32),
            pltpu.VMEM((GH, 1, BLK), F32),
        ],
        compiler_params=pltpu.CompilerParams(vmem_limit_bytes=48 * 2**20),
        name="attend",
    )(pos, sel, query, key, value_t)


COLS = 512


def project_kernel(parts_ref, weight_ref, out_ref, held):
    @pl.when(pl.program_id(0) == 0)
    def _():
        for group in range(N_TP):
            for head in range(GH):
                logs = []
                for source in range(NX):
                    stats = parts_ref[source * N_TP + group, pl.ds(GH * HD, STAT), :].astype(F32)
                    own = stats[head * 8 : head * 8 + 8]
                    logs.append(own[0:1] + own[1:2] + own[2:3])
                best = functools.reduce(jnp.maximum, logs)
                shares = [jnp.exp2(one - best) for one in logs]
                inverse = 1.0 / functools.reduce(jnp.add, shares)
                total = jnp.zeros((HD, ROWS), F32)
                for source in range(NX):
                    part = parts_ref[source * N_TP + group, pl.ds(head * HD, HD), :]
                    total = total + part.astype(F32) * shares[source]
                held[:, pl.ds((group * GH + head) * HD, HD)] = (total * inverse).T.astype(BF16)

    out_ref[...] = dot(held[...], weight_ref[...], ((1,), (0,))).astype(BF16)


def project(parts, weight):
    depth = weight.shape[0]
    return pl.pallas_call(
        project_kernel,
        out_shape=jax.ShapeDtypeStruct((ROWS, D), BF16),
        grid=(D // COLS,),
        in_specs=[
            pl.BlockSpec(parts.shape, lambda n: (0, 0, 0)),
            pl.BlockSpec((depth, COLS), lambda n: (0, n)),
        ],
        out_specs=pl.BlockSpec((ROWS, COLS), lambda n: (0, n)),
        scratch_shapes=[pltpu.VMEM((ROWS, depth), BF16)],
        compiler_params=pltpu.CompilerParams(vmem_limit_bytes=32 * 2**20),
        name="project",
    )(parts, weight)


def local(query, key, value, selections, out_weight):
    pos = jnp.stack([lax.axis_index("z"), lax.axis_index("x")]).astype(jnp.int32)
    keys = lax.all_gather(key, "z", tiled=True)
    values_t = lax.all_gather(value.T, "z")
    queries = lax.all_gather(query, "x", tiled=True)
    weight = lax.all_gather(out_weight, ("y", "c"), tiled=True)
    parts = attend(pos, selections.reshape(-1), queries, keys, values_t)
    parts = lax.all_to_all(parts, ("x", "y", "c"), split_axis=0, concat_axis=0, tiled=True)
    return project(parts, weight)


def solution(mesh):
    grid = Mesh(mesh.devices.reshape(NZ, NX, NY, NC), ("z", "x", "y", "c"))
    tokens = P(("z", "x"), ("y", "c"))
    in_specs = (tokens, tokens, tokens, P(None, ("y", "c"), None), P(("y", "c"), None))
    out_specs = P(("z", "x", "y", "c"), None)
    return jax.shard_map(local, mesh=grid, in_specs=in_specs, out_specs=out_specs, check_vma=False)
```

time: 1010 us -> 297 us (0.29)
  waiting for transfers between devices: 419 us -> 212 us
  loops' own time: 195 us -> 0 us
  local copies, waits for them, and re-layouts: 183 us -> 14.6 us
  other arithmetic: 81.6 us -> 0.08 us
  matrix products: 71.5 us -> 0 us
  Pallas kernels: 0 us -> 18.1 us
  starting transfers between devices: 17.6 us -> 0.12 us
  blocking collectives: 23.7 us -> 38.7 us
    all_to_all x2 -> x0, waiting for transfers between devices: 361 us -> none  [the longest x1 184 us: local(): lax.all_to_all(sent_queries, 'ctx', split_axis=0, concat_axis=0, tiled=True)]
    all_gather x0 -> x4, waiting for transfers between devices: none -> 209 us  [the longest x1 62.4 us: local(): values_t = lax.all_gather(value.T, 'z')]
    another operation x33 -> x0, loops' own time: 195 us -> none  [the longest x32 129 us: single_pair(): return lax.cond(usable[source_slot, group_pos], compute_part, skip_part)]
    dynamic_slice x115 -> x0, local copies, waits for them, and re-layouts: 101 us -> none  [the longest x32 40.3 us: pair_loop(): lax.map(single_pair, jnp.arange(slot_count * group_count, dtype=jnp.int32))]
    dot_general x57 -> x0, matrix products: 71.5 us -> none  [the longest x28 34.4 us: block_terms(): jnp.einsum('hqk,khd->qhd', weights.astype(jnp.bfloat16), value_heads, pre...]
    reduce_scatter x1 -> x0, waiting for transfers between devices: 58.7 us -> none  [local(): lax.psum_scatter(jnp.dot(attention, out_weight, preferred_element_type=jn...]
    dynamic_update_slice x96 -> x0, local copies, waits for them, and re-layouts: 45.9 us -> none  [pair_loop(): lax.map(single_pair, jnp.arange(slot_count * group_count, dtype=jnp.int32))]
    reduce_sum x33 -> x0, other arithmetic: 40.9 us -> none  [the longest x28 29.4 us: block_terms(): totals = jnp.sum(weights, axis=-1)]
  transfers between devices with their start and end apart: 3 -> 4, of which waited for: 3 -> 4; matrix products, arithmetic and copies ran while one was open for 1% -> 2% of each run, Pallas kernels for 0% -> 4%
where the time goes in v1:
time: 297 us
  waiting for transfers between devices  212 us (71%)
  blocking collectives  38.7 us (13%)
  Pallas kernels  18.1 us (6%)
  local copies, waits for them, and re-layouts  14.6 us (5%)
  between operations  13.1 us (4%)
    all_gather x1, waiting for transfers between devices, local(): values_t = lax.all_gather(value.T, 'z')  62.4 us
    all_gather x1, waiting for transfers between devices, local(): weight = lax.all_gather(out_weight, ('y', 'c'), tiled=True)  60.2 us
    all_gather x1, waiting for transfers between devices, local(): keys = lax.all_gather(key, 'z', tiled=True)  56.7 us
    all_to_all x1, blocking collectives, local(): lax.all_to_all(parts, ('x', 'y', 'c'), split_axis=0, concat_axis=0, tiled...  38.7 us
    all_gather x1, waiting for transfers between devices, local(): queries = lax.all_gather(query, 'x', tiled=True)  30.2 us
    pallas_call x1, Pallas kernels, attend(): pl.pallas_call(attend_kernel, out_shape=jax.ShapeDtypeStruct((NX * N_TP,...  11.7 us
    unnamed x5, local copies, waits for them, and re-layouts  8.13 us
    all_gather x1, local copies, waits for them, and re-layouts, local(): values_t = lax.all_gather(value.T, 'z')  6.36 us
  transfers between devices with their start and end apart: 4, of which 4 were waited for; matrix products, arithmetic and copies ran while one was open for 2% of the time, Pallas kernels for 4%

profile of v1, /device:TPU:1, one launch (start us, length us, event | category | flops | bytes accessed | tf_op | source)
XLA Modules:
  0.0 296.7 jit_solution(14806946875381568491)
XLA Ops:
  6.5 0.0 all-gather.12.cloned.1.call-start
  6.5 0.7 all-gather.12.cloned.1.call-update
  7.3 0.0 all-gather.6.cloned.1.call-start
  7.3 0.7 all-gather.6.cloned.1.call-update
  8.0 0.0 all-gather.8.cloned.1.call-start
  8.1 0.7 all-gather.8.cloned.1.call-update
  8.7 0.0 all-gather.10.cloned.1.call-start
  8.8 0.5 all-gather.10.cloned.1.call-update
  9.3 0.8 copy.7
  10.1 0.1 reshape.3.sel_ref
  10.2 0.1 pad_add_fusion.pos_ref
  10.3 62.4 %all-gather.12.cloned.1.call-done = bf16[2048,1024]{0,1:T(8,128)(2,1)} async-done(((bf16[256,1024]{0,1:T(8,128)(2,1)}), bf16[2048,1024]{0,1:T(8,128)(2,1)}) %all-gather.12.cloned.1.call-update) | async-done | bytes 4194320 | tf_op jit(solution)/shard_map/all_gather | solution.py:177
  72.6 6.4 %copy.8 = bf16[2048,1024]{1,0:T(8,128)(2,1)} copy(bf16[2048,1024]{0,1:T(8,128)(2,1)} %all-gather.12.cloned.1.call-done) | data formatting | bytes 8388608 | tf_op jit(solution)/shard_map/all_gather | solution.py:177
  79.0 30.2 %all-gather.6.cloned.1.call-done.q_ref = bf16[4096,256]{1,0:T(8,128)(2,1)} async-done(((bf16[1024,256]{1,0:T(8,128)(2,1)}), bf16[4096,256]{1,0:T(8,128)(2,1)}) %all-gather.6.cloned.1.call-update) | async-done | bytes 2097168 | tf_op jit(solution)/shard_map/all_gather | solution.py:178
  109.1 56.7 %all-gather.8.cloned.1.call-done.k_ref = bf16[8192,256]{1,0:T(8,128)(2,1)} async-done(((bf16[1024,256]{1,0:T(8,128)(2,1)}), bf16[8192,256]{1,0:T(8,128)(2,1)}) %all-gather.8.cloned.1.call-update) | async-done | bytes 4194320 | tf_op jit(solution)/shard_map/all_gather | solution.py:176
  165.8 0.0 copy-start.1
  165.8 1.6 copy-done.1
  167.4 11.7 %attend.1 = bf16[32,272,128]{2,1,0:T(8,128)(2,1)S(1)} custom-call(s32[2]{0:T(128)S(1)} %pad_add_fusion.pos_ref, s32[512]{0:T(512)S(1)} %reshape.3.sel_ref, bf16[4096,256]{1,0:T(8,128)(2,1)S(1)} %copy-done.1, bf16[8192,256]{1,0:T(8,128)(2,1)} %all-gather.8.cloned.1.call-done.k_ref, bf16[8,256,1024]{2,1,0:T(8,128)(2,1)} %bitcast.6), custom_call_target="tpu_custom_call" | custom-call | tf_op jit(solution)/shard_map/attend/pallas_call | solution.py:117
  179.1 38.7 %all_to_all.5.parts_ref = bf16[32,272,128]{2,1,0:T(8,128)(2,1)S(1)} all-to-all(bf16[32,272,128]{2,1,0:T(8,128)(2,1)S(1)} %attend.1), channel_id=1, replica_groups=mesh['z'=8,'x'=4,'y'=4,'c'=2] {'x','y','c'}, dimensions={0} | all-to-all | bytes 4456448 | tf_op jit(solution)/shard_map/all_to_all | solution.py:181
  217.8 60.2 %all-gather.10.cloned.1.call-done.weight_ref = bf16[2048,4096]{1,0:T(8,128)(2,1)} async-done(((bf16[256,4096]{1,0:T(8,128)(2,1)}), bf16[2048,4096]{1,0:T(8,128)(2,1)}) %all-gather.10.cloned.1.call-update) | async-done | bytes 16777232 | tf_op jit(solution)/shard_map/all_gather | solution.py:179
  278.0 0.0 copy-start
  278.0 5.8 %copy-done = bf16[2048,4096]{1,0:T(8,128)(2,1)S(1)} copy-done((bf16[2048,4096]{1,0:T(8,128)(2,1)S(1)}, bf16[2048,4096]{1,0:T(8,128)(2,1)}, u32[]{:S(2)}) %copy-start) | copy-done | bytes 16777240
  283.8 6.3 %project.1 = bf16[128,4096]{1,0:T(8,128)(2,1)} custom-call(bf16[32,272,128]{2,1,0:T(8,128)(2,1)S(1)} %all_to_all.5.parts_ref, bf16[2048,4096]{1,0:T(8,128)(2,1)S(1)} %copy-done), custom_call_target="tpu_custom_call" | custom-call | tf_op jit(solution)/shard_map/project/pallas_call | solution.py:159
Async XLA Ops:
  6.5 66.1 %all-gather.12.cloned.1.call-start = ((), (), s32[]{:S(2)}) async-start(), calls=%async_computation.4 | async-start | bytes 4718592 | tf_op jit(solution)/shard_map/all_gather | solution.py:177
  7.3 101.9 %all-gather.6.cloned.1.call-start = ((), (), s32[]{:S(2)}) async-start(), calls=%async_computation.1 | async-start | bytes 2621440 | tf_op jit(solution)/shard_map/all_gather | solution.py:178
  8.0 157.8 %all-gather.8.cloned.1.call-start = ((), (), s32[]{:S(2)}) async-start(), calls=%async_computation.2 | async-start | bytes 4718592 | tf_op jit(solution)/shard_map/all_gather | solution.py:176
  8.7 269.3 %all-gather.10.cloned.1.call-start = ((), (), s32[]{:S(2)}) async-start(), calls=%async_computation.3 | async-start | bytes 18874368 | tf_op jit(solution)/shard_map/all_gather | solution.py:179
  165.8 1.6 copy-start.1
  278.0 5.8 %copy-start = (bf16[2048,4096]{1,0:T(8,128)(2,1)S(1)}, bf16[2048,4096]{1,0:T(8,128)(2,1)}, u32[]{:S(2)}) copy-start(bf16[2048,4096]{1,0:T(8,128)(2,1)} %all-gather.10.cloned.1.call-done.weight_ref) | copy-start | bytes 50331652
Sparse Core Ops, SparseCore 0:
  9.1 63.5 all-gather.11
  74.4 34.6 all-gather.5
  110.9 54.8 all-gather.7
  167.6 110.4 all-gather.9

commit v2 on v1

v2 whole, which is shorter than its diff:
```python
import functools
import math

import jax
import jax.numpy as jnp
from jax import lax
from jax.experimental import pallas as pl
from jax.experimental.pallas import tpu as pltpu
from jax.sharding import Mesh, PartitionSpec as P

HD = 128
BLK = 512
SEL = 8
GH = 2
NZ, NX, NY, NC = 8, 4, 4, 2
N_TP = NY * NC
LOCAL = 2
TOK = LOCAL * BLK
ROWS = TOK // N_TP
STAT = 16
MSG = HD + STAT
D = 4096
NEG = -1e30
SCALE = math.log2(math.e) / math.sqrt(HD)
F32 = jnp.float32
BF16 = jnp.bfloat16

UP = (0, 1, 0, 1, 0, 1, 0, 3, 2, 3, 2, 3, 2, 3)
DOWN = (1, 0, 1, 0, 1, 0, 1, 2, 3, 2, 3, 2, 3, 2)


def dot(a, b, dims):
    return lax.dot_general(a, b, (dims, ((), ())), preferred_element_type=F32)


def split_kernel(k_ref, v_ref, *outs):
    for head in range(GH):
        cols = pl.ds(head * HD, HD)
        outs[2 * head][...] = k_ref[:, cols]
        outs[2 * head + 1][...] = v_ref[:, cols].T


def split_heads(key, value):
    vmem = pl.BlockSpec(memory_space=pltpu.VMEM)
    shapes = [jax.ShapeDtypeStruct((TOK, HD), BF16), jax.ShapeDtypeStruct((HD, TOK), BF16)] * GH
    return pl.pallas_call(
        split_kernel,
        out_shape=shapes,
        in_specs=[vmem, vmem],
        out_specs=[vmem] * len(shapes),
        name="split_heads",
    )(key, value)


def attend_kernel(head, planes, offsets_k, offsets_v, pos_ref, sel_ref, *refs):
    count_q = len(planes)
    queries, refs = refs[:count_q], refs[count_q:]
    keys, refs = refs[:NZ], refs[NZ:]
    values, refs = refs[:NZ], refs[NZ:]
    out_ref, q_buf, k_buf, v_buf, stage, acc, top, tot, listed, sems, out_sems = refs[-11:]
    my_z = pos_ref[0]
    my_x = pos_ref[1]
    copies = []
    for at, ref in enumerate(queries):
        copies.append(pltpu.make_async_copy(ref.at[:, pl.ds(head * HD, HD)], q_buf.at[at], sems.at[at]))
    for at, (off, ref) in enumerate(zip(offsets_k, keys)):
        slot = lax.rem(my_z + NZ - off, NZ)
        copies.append(pltpu.make_async_copy(ref, k_buf.at[slot], sems.at[count_q + at]))
    for at, (off, ref) in enumerate(zip(offsets_v, values)):
        slot = lax.rem(my_z + NZ - off, NZ)
        copies.append(pltpu.make_async_copy(ref, v_buf.at[slot], sems.at[count_q + NZ + at]))
    for copy in copies:
        copy.start()
    for copy in copies:
        copy.wait()

    def step(slots, query, diagonal):
        places = [(slot // LOCAL, pl.multiple_of(slot % LOCAL * BLK, BLK)) for slot in slots]
        scores = [dot(k_buf[z_at, pl.ds(first, BLK), :], query, ((1,), (1,))) for z_at, first in places]
        if diagonal:
            key_at = lax.broadcasted_iota(jnp.int32, (BLK, BLK), 0)
            query_at = lax.broadcasted_iota(jnp.int32, (BLK, BLK), 1)
            scores[0] = jnp.where(key_at <= query_at, scores[0], NEG)
        old = top[...]
        new = functools.reduce(jnp.maximum, [old] + [jnp.max(one, axis=0, keepdims=True) for one in scores])
        fade = jnp.exp2((old - new) * SCALE)
        top[...] = new
        both = None
        for one, (z_at, first) in zip(scores, places):
            weights = jnp.exp2((one - new) * SCALE).astype(BF16)
            value = jnp.concatenate([v_buf[z_at, :, pl.ds(first, BLK)], jnp.ones((16, BLK), BF16)], axis=0)
            more = dot(value, weights, ((1,), (0,)))
            both = more if both is None else both + more
        tot[...] = tot[...] * fade + both[HD : HD + 1]
        acc[...] = acc[...] * fade + both[:HD]

    def query_block(index, carry):
        plane = index // LOCAL
        half = index % LOCAL
        x_at = lax.rem(my_x + NX - planes[0] - plane, NX)
        block = (my_z * NX + x_at) * LOCAL + half
        acc[...] = jnp.zeros_like(acc)
        top[...] = jnp.full_like(top, NEG)
        tot[...] = jnp.zeros_like(tot)
        query = q_buf[plane, pl.ds(pl.multiple_of(half * BLK, BLK), BLK), :]

        def gather(at, count):
            key = sel_ref[block * SEL + at]
            owner = key // LOCAL
            found = (key < block) & (owner % NX == my_x)
            listed[count] = owner // NX * LOCAL + key % LOCAL
            return count + found.astype(jnp.int32)

        count = lax.fori_loop(0, SEL, gather, 0)

        @pl.when(x_at == my_x)
        def _():
            step([my_z * LOCAL + half], query, True)

        def pairs(at, c):
            step([listed[2 * at], listed[2 * at + 1]], query, False)
            return c

        lax.fori_loop(0, count // 2, pairs, 0)

        @pl.when(count % 2 == 1)
        def _():
            step([listed[count - 1]], query, False)

        pieces = BLK // ROWS
        total = tot[...]
        some = total > 0.0
        safe = jnp.where(some, total, 1.0)
        mean = (acc[...] / safe).astype(BF16)
        log_total = jnp.where(some, top[...] * SCALE + jnp.log2(safe), NEG)
        high = log_total.astype(BF16).astype(F32)
        rest = log_total - high
        mid = rest.astype(BF16).astype(F32)
        low = rest - mid
        row = lax.broadcasted_iota(jnp.int32, (STAT, BLK), 0)
        wide = (STAT, BLK)
        packed = jnp.where(
            row == 0,
            jnp.broadcast_to(high, wide),
            jnp.where(row == 1, jnp.broadcast_to(mid, wide), jnp.broadcast_to(low, wide)),
        ).astype(BF16)
        for piece in range(pieces):
            lanes = slice(piece * ROWS, (piece + 1) * ROWS)
            at = index * pieces + piece
            stage[at, pl.ds(0, HD), :] = mean[:, lanes]
            stage[at, pl.ds(HD, STAT), :] = packed[:, lanes]
        return carry

    lax.fori_loop(0, count_q * LOCAL, query_block, 0)
    copies = []
    for plane, off in enumerate(planes):
        to = out_ref.at[pl.ds(lax.rem(my_x + NX - off, NX) * N_TP, N_TP)]
        copies.append(pltpu.make_async_copy(stage.at[pl.ds(plane * N_TP, N_TP)], to, out_sems.at[plane]))
    for copy in copies:
        copy.start()
    for copy in copies:
        copy.wait()


def attend(head, planes, pos, sel, queries, keys, values, parts=None):
    smem = pl.BlockSpec(memory_space=pltpu.SMEM)
    far = pl.BlockSpec(memory_space=pltpu.HBM)
    offsets_k, keys = zip(*keys)
    offsets_v, values = zip(*values)
    arrays = [queries[at] for at in planes] + [*keys, *values] + ([] if parts is None else [parts])
    arrays = [pltpu.with_memory_space_constraint(one, pltpu.HBM) for one in arrays]
    most = len(planes) * LOCAL * (SEL + 1) * BLK * BLK
    return pl.pallas_call(
        functools.partial(attend_kernel, head, planes, offsets_k, offsets_v),
        out_shape=jax.ShapeDtypeStruct((NX * N_TP, MSG, ROWS), BF16),
        in_specs=[smem, smem] + [far] * len(arrays),
        out_specs=far,
        scratch_shapes=[
            pltpu.VMEM((len(planes), TOK, HD), BF16),
            pltpu.VMEM((NZ, TOK, HD), BF16),
            pltpu.VMEM((NZ, HD, TOK), BF16),
            pltpu.VMEM((len(planes) * N_TP, MSG, ROWS), BF16),
            pltpu.VMEM((HD, BLK), F32),
            pltpu.VMEM((1, BLK), F32),
            pltpu.VMEM((1, BLK), F32),
            pltpu.SMEM((SEL + 1,), jnp.int32),
            pltpu.SemaphoreType.DMA((len(planes) + 2 * NZ,)),
            pltpu.SemaphoreType.DMA((len(planes),)),
        ],
        input_output_aliases={} if parts is None else {1 + len(arrays): 0},
        compiler_params=pltpu.CompilerParams(vmem_limit_bytes=16 * 2**20),
        name=f"attend{head}",
        cost_estimate=pl.CostEstimate(flops=4 * HD * most, transcendentals=most, bytes_accessed=12 * 2**20),
    )(pos, sel, *arrays)


COLS = 1024


def project_kernel(has_base, parts_ref, weight_ref, *refs):
    base_ref = refs[0] if has_base else None
    out_ref, held = refs[-2:]

    @pl.when(pl.program_id(0) == 0)
    def _():
        for group in range(N_TP):
            logs = []
            for source in range(NX):
                stats = parts_ref[source * N_TP + group, pl.ds(HD, STAT), :].astype(F32)
                logs.append(stats[0:1] + stats[1:2] + stats[2:3])
            best = functools.reduce(jnp.maximum, logs)
            shares = [jnp.exp2(one - best) for one in logs]
            inverse = 1.0 / functools.reduce(jnp.add, shares)
            total = jnp.zeros((HD, ROWS), F32)
            for source in range(NX):
                part = parts_ref[source * N_TP + group, pl.ds(0, HD), :]
                total = total + part.astype(F32) * shares[source]
            held[:, pl.ds(group * HD, HD)] = (total * inverse).T.astype(BF16)

    result = dot(held[...], weight_ref[...].reshape(N_TP * HD, COLS), ((1,), (0,)))
    if has_base:
        result = base_ref[...] + result
    out_ref[...] = result.astype(out_ref.dtype)


def project(head, parts, weight, base, dtype):
    depth = N_TP * HD
    piece = pl.BlockSpec((ROWS, COLS), lambda n: (0, n))
    return pl.pallas_call(
        functools.partial(project_kernel, base is not None),
        out_shape=jax.ShapeDtypeStruct((ROWS, D), dtype),
        grid=(D // COLS,),
        in_specs=[
            pl.BlockSpec(parts.shape, lambda n: (0, 0, 0)),
            pl.BlockSpec((N_TP, 1, HD, COLS), lambda n: (0, head, 0, n)),
        ]
        + ([piece] if base is not None else []),
        out_specs=piece,
        scratch_shapes=[pltpu.VMEM((ROWS, depth), BF16)],
        compiler_params=pltpu.CompilerParams(vmem_limit_bytes=16 * 2**20),
        cost_estimate=pl.CostEstimate(flops=2 * ROWS * depth * D, transcendentals=0, bytes_accessed=12 * 2**20),
        name=f"project{head}",
    )(parts, pltpu.with_memory_space_constraint(weight, pltpu.HBM), *([base] if base is not None else []))


def send(array, axis, count, by):
    return lax.ppermute(array, axis, [(at, (at + by) % count) for at in range(count)])


def local(query, key, value, selections, out_weight):
    pos = jnp.stack([lax.axis_index("z"), lax.axis_index("x")]).astype(jnp.int32)
    sel = selections.reshape(-1)
    queries = [query] + [send(query, "x", NX, by) for by in range(1, NX)]
    weight = lax.all_gather(out_weight.reshape(GH, HD, D), ("y", "c"))
    arrays = split_heads(key, value)
    found = [{0: array} for array in arrays]
    sent = {1: [], -1: []}
    base = None

    def travel(first, last, after=None):
        for turn in range(first, last):
            for sign, turns in ((1, UP), (-1, DOWN)):
                at = turns[turn]
                step = 1 + turns[:turn].count(at)
                source = found[at][sign * (step - 1)]
                if step == 1 and turn > 1:
                    source = lax.optimization_barrier((source, sent[sign][-2]))[0]
                if after is not None:
                    source = lax.optimization_barrier((source, after))[0]
                moved = send(source, "z", NZ, sign)
                found[at][sign * step] = moved
                sent[sign].append(moved)

    def head_parts(head, planes, after=None, parts=None):
        keys, values = (list(found[2 * head + at].items()) for at in range(2))
        if after is not None:
            held = ([array for _, array in keys], after)
            keys = list(zip([off for off, _ in keys], lax.optimization_barrier(held)[0]))
        return attend(head, planes, pos, sel, queries, keys, values, parts)

    def swap(parts):
        return lax.all_to_all(parts, ("x", "y", "c"), split_axis=0, concat_axis=0, tiled=True)

    def turn(at):
        return [sent[sign][at] for sign in (1, -1)]

    travel(0, 4)
    travel(4, 5, queries[1:])
    travel(5, 10)
    parts = head_parts(0, (0, 1), turn(7))
    travel(10, 11, parts)
    travel(11, 12)
    parts = head_parts(0, (2, 3), turn(9), parts)
    travel(12, 13, parts)
    travel(13, 14)
    parts = lax.optimization_barrier((parts, turn(11)))[0]
    base = project(0, swap(parts), weight, None, F32)
    return project(1, swap(head_parts(1, (0, 1, 2, 3))), weight, base, BF16)


def solution(mesh):
    grid = Mesh(mesh.devices.reshape(NZ, NX, NY, NC), ("z", "x", "y", "c"))
    tokens = P(("z", "x"), ("y", "c"))
    in_specs = (tokens, tokens, tokens, P(None, ("y", "c"), None), P(("y", "c"), None))
    out_specs = P(("z", "x", "y", "c"), None)
    return jax.shard_map(local, mesh=grid, in_specs=in_specs, out_specs=out_specs, check_vma=False)
```

time: 297 us -> 169 us (0.57)
  waiting for transfers between devices: 212 us -> 49.6 us
  starting transfers between devices: 0.12 us -> 66.3 us
  blocking collectives: 38.7 us -> 0 us
  Pallas kernels: 18.1 us -> 36.1 us
  local copies, waits for them, and re-layouts: 14.6 us -> 4.18 us
    all_gather x4 -> x1, waiting for transfers between devices: 209 us -> 0.02 us  [local(): weight = lax.all_gather(out_weight.reshape(GH, HD, D), ('y', 'c'))]
    ppermute x0 -> x31, starting transfers between devices: none -> 49.6 us  [send(): lax.ppermute(array, axis, [(at, (at + by) % count) for at in range(count)])]
    all_to_all x1 -> x0, blocking collectives: 38.7 us -> none  [local(): lax.all_to_all(parts, ('x', 'y', 'c'), split_axis=0, concat_axis=0, tiled...]
    ppermute x0 -> x31, waiting for transfers between devices: none -> 28.5 us  [send(): lax.ppermute(array, axis, [(at, (at + by) % count) for at in range(count)])]
    all_to_all x0 -> x2, waiting for transfers between devices: none -> 20.4 us  [swap(): lax.all_to_all(parts, ('x', 'y', 'c'), split_axis=0, concat_axis=0, tiled...]
    pallas_call x2 -> x6, Pallas kernels: 18.1 us -> 36.1 us  [the longest x3 22 us: attend(): pl.pallas_call(functools.partial(attend_kernel, head, planes, offsets_k,...]
    all_to_all x0 -> x2, starting transfers between devices: none -> 16.8 us  [swap(): lax.all_to_all(parts, ('x', 'y', 'c'), split_axis=0, concat_axis=0, tiled...]
    all_gather x1 -> x0, local copies, waits for them, and re-layouts: 6.36 us -> none  [local(): values_t = lax.all_gather(value.T, 'z')]
  transfers between devices with their start and end apart: 4 -> 34, of which waited for: 4 -> 12; matrix products, arithmetic and copies ran while one was open for 2% -> 0% of each run, Pallas kernels for 4% -> 17%
where the time goes in v2:
time: 169 us; the launch traced here: 170 us
  starting transfers between devices  66.3 us (39%)
  waiting for transfers between devices  49.6 us (29%)
  Pallas kernels  36.1 us (21%)
  between operations  13.7 us (8%)
  local copies, waits for them, and re-layouts  4.18 us (2%)
    ppermute x31, starting transfers between devices, send(): lax.ppermute(array, axis, [(at, (at + by) % count) for at in range(count)])  49.6 us
    ppermute x31, waiting for transfers between devices, send(): lax.ppermute(array, axis, [(at, (at + by) % count) for at in range(count)])  28.5 us
    pallas_call x3, Pallas kernels, attend(): pl.pallas_call(functools.partial(attend_kernel, head, planes, offsets_k,...  22 us
    all_to_all x2, waiting for transfers between devices, swap(): lax.all_to_all(parts, ('x', 'y', 'c'), split_axis=0, concat_axis=0, tiled...  20.4 us
    all_to_all x2, starting transfers between devices, swap(): lax.all_to_all(parts, ('x', 'y', 'c'), split_axis=0, concat_axis=0, tiled...  16.8 us
    pallas_call x2, Pallas kernels, project(): pl.pallas_call(functools.partial(project_kernel, base is not None), out_s...  11.7 us
    unnamed x61, local copies, waits for them, and re-layouts  4.09 us
  transfers between devices with their start and end apart: 34, of which 12 were waited for; matrix products, arithmetic and copies ran while one was open for 0% of the time, Pallas kernels for 17%

profile of v2, /device:TPU:1, one launch (start us, length us, event | category | flops | bytes accessed | tf_op | source)
XLA Modules:
  0.0 169.9 jit_solution(3201273736124665436)
XLA Ops:
  7.3 2.3 %split_heads.1 = (bf16[1024,128]{1,0:T(8,128)(2,1)}, bf16[128,1024]{1,0:T(8,128)(2,1)}, bf16[1024,128]{1,0:T(8,128)(2,1)}, bf16[128,1024]{1,0:T(8,128)(2,1)}) custom-call(bf16[1024,256]{1,0:T(8,128)(2,1)} %k_ref.1, bf16[1024,256]{1,0:T(8,128)(2,1)} %v_ref.1), custom_call_target="tpu_custom_call" | custom-call | tf_op jit(solution)/shard_map/split_heads/pallas_call | solution.py:46
  9.5 6.4 %collective-permute-start.3 = (bf16[1024,128]{1,0:T(8,128)(2,1)}, bf16[1024,128]{1,0:T(8,128)(2,1)S(1)}, u32[]{:S(2)}, u32[]{:S(2)}) collective-permute-start(bf16[1024,128]{1,0:T(8,128)(2,1)} %get-tuple-element.54.refs_2_), channel_id=1, source_target_pairs={{0,224},{32,0},{64,32},{96,64},{128,96},{160,128},{192,160},{224,1... | collective-permute-start | bytes 786440 | tf_op jit(solution)/shard_map/ppermute | solution.py:247
  17.2 2.5 %collective-permute-start.1 = (bf16[1024,256]{1,0:T(8,128)(2,1)S(1)}, bf16[1024,256]{1,0:T(8,128)(2,1)S(1)}, u32[]{:S(2)}, u32[]{:S(2)}) collective-permute-start(bf16[1024,256]{1,0:T(8,128)(2,1)S(1)} %copy-done.2), channel_id=1, source_target_pairs={{0,16},{8,24},{16,0},{24,8},{1,17},{9,25},{17,1},{25,9},{2,18},{10... | collective-permute-start | bytes 1572872 | tf_op jit(solution)/shard_map/ppermute | solution.py:247
  19.6 1.6 collective-permute-done.3.refs_4_
  21.2 3.3 %collective-permute-start.17 = (bf16[128,1024]{1,0:T(8,128)(2,1)}, bf16[128,1024]{1,0:T(8,128)(2,1)S(1)}, u32[]{:S(2)}, u32[]{:S(2)}) collective-permute-start(bf16[128,1024]{1,0:T(8,128)(2,1)} %get-tuple-element.42.refs_10_), channel_id=1, source_target_pairs={{0,224},{32,0},{64,32},{96,64},{128,96},{160,128},{192,160},{224,1... | collective-permute-start | bytes 786440 | tf_op jit(solution)/shard_map/ppermute | solution.py:247
  24.6 2.5 %collective-permute-start.2 = (bf16[1024,256]{1,0:T(8,128)(2,1)S(1)}, bf16[1024,256]{1,0:T(8,128)(2,1)S(1)}, u32[]{:S(2)}, u32[]{:S(2)}) collective-permute-start(bf16[1024,256]{1,0:T(8,128)(2,1)S(1)} %copy-done.2), channel_id=1, source_target_pairs={{0,24},{8,0},{16,8},{24,16},{1,25},{9,1},{17,9},{25,17},{2,26},{10... | collective-permute-start | bytes 1572872 | tf_op jit(solution)/shard_map/ppermute | solution.py:247
  27.0 2.8 %collective-permute-done.13.refs_12_ = bf16[128,1024]{1,0:T(8,128)(2,1)S(1)} collective-permute-done((bf16[128,1024]{1,0:T(8,128)(2,1)}, bf16[128,1024]{1,0:T(8,128)(2,1)S(1)}, u32[]{:S(2)}, u32[]{:S(2)}) %collective-permute-start.13) | collective-permute-done | bytes 262176 | tf_op jit(solution)/shard_map/ppermute | solution.py:247
  29.9 1.5 collective-permute-start.8
  31.4 10.4 %collective-permute-done.1.refs_0_.refs_2_ = bf16[1024,256]{1,0:T(8,128)(2,1)S(1)} collective-permute-done((bf16[1024,256]{1,0:T(8,128)(2,1)S(1)}, bf16[1024,256]{1,0:T(8,128)(2,1)S(1)}, u32[]{:S(2)}, u32[]{:S(2)}) %collective-permute-start.1) | collective-permute-done | bytes 524320 | tf_op jit(solution)/shard_map/ppermute | solution.py:247
  41.9 2.4 %collective-permute-start.18 = (bf16[128,1024]{1,0:T(8,128)(2,1)S(1)}, bf16[128,1024]{1,0:T(8,128)(2,1)S(1)}, u32[]{:S(2)}, u32[]{:S(2)}) collective-permute-start(bf16[128,1024]{1,0:T(8,128)(2,1)S(1)} %collective-permute-done.17.refs_11_), channel_id=1, source_target_pairs={{0,224},{32,0},{64,32},{96,64},{128,96},{160,128},{192,160},{224,1... | collective-permute-start | bytes 786440 | tf_op jit(solution)/shard_map/ppermute | solution.py:247
  44.4 1.5 collective-permute-start.9
  45.9 2.0 %collective-permute-done.18.refs_13_ = bf16[128,1024]{1,0:T(8,128)(2,1)S(1)} collective-permute-done((bf16[128,1024]{1,0:T(8,128)(2,1)S(1)}, bf16[128,1024]{1,0:T(8,128)(2,1)S(1)}, u32[]{:S(2)}, u32[]{:S(2)}) %collective-permute-start.18) | collective-permute-done | bytes 262176 | tf_op jit(solution)/shard_map/ppermute | solution.py:247
  47.9 3.3 %collective-permute-start.19 = (bf16[128,1024]{1,0:T(8,128)(2,1)S(1)}, bf16[128,1024]{1,0:T(8,128)(2,1)}, u32[]{:S(2)}, u32[]{:S(2)}) collective-permute-start(bf16[128,1024]{1,0:T(8,128)(2,1)S(1)} %collective-permute-done.18.refs_13_), channel_id=1, source_target_pairs={{0,224},{32,0},{64,32},{96,64},{128,96},{160,128},{192,160},{224,1... | collective-permute-start | bytes 786440 | tf_op jit(solution)/shard_map/ppermute | solution.py:247
  51.2 2.3 %collective-permute-done.5.refs_8_ = bf16[1024,128]{1,0:T(8,128)(2,1)S(1)} collective-permute-done((bf16[1024,128]{1,0:T(8,128)(2,1)S(1)}, bf16[1024,128]{1,0:T(8,128)(2,1)S(1)}, u32[]{:S(2)}, u32[]{:S(2)}) %collective-permute-start.5) | collective-permute-done | bytes 262176 | tf_op jit(solution)/shard_map/ppermute | solution.py:247
  53.5 3.3 %collective-permute-start.6 = (bf16[1024,128]{1,0:T(8,128)(2,1)}, bf16[1024,128]{1,0:T(8,128)(2,1)S(1)}, u32[]{:S(2)}, u32[]{:S(2)}) collective-permute-start(bf16[1024,128]{1,0:T(8,128)(2,1)} %get-tuple-element.40.refs_4_), channel_id=1, source_target_pairs={{0,224},{32,0},{64,32},{96,64},{128,96},{160,128},{192,160},{224,1... | collective-permute-start | bytes 786440 | tf_op jit(solution)/shard_map/ppermute | solution.py:247
  57.6 1.6 collective-permute-done.19.refs_15_
  59.1 3.3 %collective-permute-start.20 = (bf16[128,1024]{1,0:T(8,128)(2,1)}, bf16[128,1024]{1,0:T(8,128)(2,1)}, u32[]{:S(2)}, u32[]{:S(2)}) collective-permute-start(bf16[128,1024]{1,0:T(8,128)(2,1)} %collective-permute-done.19.refs_15_), channel_id=1, source_target_pairs={{0,224},{32,0},{64,32},{96,64},{128,96},{160,128},{192,160},{224,1... | collective-permute-start | bytes 786440 | tf_op jit(solution)/shard_map/ppermute | solution.py:247
  64.8 1.9 %collective-permute-done.16.refs_13_ = bf16[128,1024]{1,0:T(8,128)(2,1)S(1)} collective-permute-done((bf16[128,1024]{1,0:T(8,128)(2,1)}, bf16[128,1024]{1,0:T(8,128)(2,1)S(1)}, u32[]{:S(2)}, u32[]{:S(2)}) %collective-permute-start.16) | collective-permute-done | bytes 262176 | tf_op jit(solution)/shard_map/ppermute | solution.py:247
  66.7 3.7 %collective-permute-done.20.refs_17_ = bf16[128,1024]{1,0:T(8,128)(2,1)} collective-permute-done((bf16[128,1024]{1,0:T(8,128)(2,1)}, bf16[128,1024]{1,0:T(8,128)(2,1)}, u32[]{:S(2)}, u32[]{:S(2)}) %collective-permute-start.20) | collective-permute-done | bytes 262176 | tf_op jit(solution)/shard_map/ppermute | solution.py:247
  70.4 3.3 %collective-permute-start.26 = (bf16[128,1024]{1,0:T(8,128)(2,1)}, bf16[128,1024]{1,0:T(8,128)(2,1)S(1)}, u32[]{:S(2)}, u32[]{:S(2)}) collective-permute-start(bf16[128,1024]{1,0:T(8,128)(2,1)} %get-tuple-element.63.refs_12_), channel_id=1, source_target_pairs={{0,224},{32,0},{64,32},{96,64},{128,96},{160,128},{192,160},{224,1... | collective-permute-start | bytes 786440 | tf_op jit(solution)/shard_map/ppermute | solution.py:247
  75.2 6.3 %attend0.2.refs_18_ = bf16[32,144,128]{2,1,0:T(8,128)(2,1)S(1)} custom-call(s32[2]{0:T(128)S(1)} %pad_add_fusion.pos_ref, s32[512]{0:T(512)S(1)} %reshape.3.sel_ref, bf16[1024,256]{1,0:T(8,128)(2,1)} %refs_0_.3, bf16[1024,256]{1,0:T(8,128)(2,1)} %copy-done.3, bf16[1024,128]{1,0:T(8,128)(2,1)} %get-tuple-element.54.refs_2_, bf16[1024,128]{1,0:T(8,128)(2,1)} %copy-done.7, ...), custom_call_target="tpu_custom_call" | custom-call | flops 4831838208 | bytes 12582912 | tf_op jit(solution)/shard_map/attend0/pallas_call | solution.py:173
  83.4 4.3 %collective-permute-start.27 = (bf16[128,1024]{1,0:T(8,128)(2,1)S(1)}, bf16[128,1024]{1,0:T(8,128)(2,1)S(1)}, u32[]{:S(2)}, u32[]{:S(2)}) collective-permute-start(bf16[128,1024]{1,0:T(8,128)(2,1)S(1)} %collective-permute-done.26.refs_14_), channel_id=1, source_target_pairs={{0,224},{32,0},{64,32},{96,64},{128,96},{160,128},{192,160},{224,1... | collective-permute-start | bytes 786440 | tf_op jit(solution)/shard_map/ppermute | solution.py:247
  87.8 1.4 collective-permute-start.22
  89.2 6.2 %attend0.3 = bf16[32,144,128]{2,1,0:T(8,128)(2,1)} custom-call(s32[2]{0:T(128)S(1)} %pad_add_fusion.pos_ref, s32[512]{0:T(512)S(1)} %reshape.3.sel_ref, bf16[1024,256]{1,0:T(8,128)(2,1)} %copy-done.4, bf16[1024,256]{1,0:T(8,128)(2,1)} %copy-done.5, bf16[1024,128]{1,0:T(8,128)(2,1)} %get-tuple-element.54.refs_2_, ...), custom_call_target="tpu_custom_call", output_to_operand_aliasing={{}: (20, {})} | custom-call | flops 4831838208 | bytes 12582912 | tf_op jit(solution)/shard_map/attend0/pallas_call | solution.py:173
  96.3 4.7 %collective-permute-start.29 = (bf16[128,1024]{1,0:T(8,128)(2,1)S(1)}, bf16[128,1024]{1,0:T(8,128)(2,1)S(1)}, u32[]{:S(2)}, u32[]{:S(2)}) collective-permute-start(bf16[128,1024]{1,0:T(8,128)(2,1)S(1)} %collective-permute-done.27.refs_16_), channel_id=1, source_target_pairs={{0,224},{32,0},{64,32},{96,64},{128,96},{160,128},{192,160},{224,1... | collective-permute-start | bytes 786440 | tf_op jit(solution)/shard_map/ppermute | solution.py:247
  103.0 12.3 %all-to-all-start.1 = ((bf16[32,144,128]{2,1,0:T(8,128)(2,1)}), bf16[32,144,128]{2,1,0:T(8,128)(2,1)S(1)}, u32[]{:S(2)}, u32[]{:S(2)}) async-start(bf16[32,144,128]{2,1,0:T(8,128)(2,1)} %attend0.3), calls=%async_computation.1 | async-start | bytes 2359296 | tf_op jit(solution)/shard_map/all_to_all | solution.py:282
  116.9 9.5 %attend1.1 = bf16[32,144,128]{2,1,0:T(8,128)(2,1)} custom-call(s32[2]{0:T(128)S(1)} %pad_add_fusion.pos_ref, s32[512]{0:T(512)S(1)} %reshape.3.sel_ref, bf16[1024,256]{1,0:T(8,128)(2,1)} %refs_0_.3, bf16[1024,256]{1,0:T(8,128)(2,1)} %copy-done.3, bf16[1024,256]{1,0:T(8,128)(2,1)} %copy-done.4, bf16[1024,256]{1,0:T(8,128)(2,1)} %copy-done.5, ...), custom_call_target="tpu_custom_call" | custom-call | flops 9663676416 | bytes 12582912 | tf_op jit(solution)/shard_map/attend1/pallas_call | solution.py:173
  126.5 7.2 %all-to-all-done.1.parts_ref = bf16[32,144,128]{2,1,0:T(8,128)(2,1)S(1)} async-done(((bf16[32,144,128]{2,1,0:T(8,128)(2,1)}), bf16[32,144,128]{2,1,0:T(8,128)(2,1)S(1)}, u32[]{:S(2)}, u32[]{:S(2)}) %all-to-all-start.1) | async-done | bytes 1179680 | tf_op jit(solution)/shard_map/all_to_all | solution.py:282
  133.7 4.5 %all-to-all-start = ((bf16[32,144,128]{2,1,0:T(8,128)(2,1)}), bf16[32,144,128]{2,1,0:T(8,128)(2,1)}, u32[]{:S(2)}, u32[]{:S(2)}) async-start(bf16[32,144,128]{2,1,0:T(8,128)(2,1)} %attend1.1), calls=%async_computation | async-start | bytes 2359296 | tf_op jit(solution)/shard_map/all_to_all | solution.py:282
  138.2 5.3 %project0.1.refs_0_ = f32[128,4096]{1,0:T(8,128)S(1)} custom-call(bf16[32,144,128]{2,1,0:T(8,128)(2,1)S(1)} %all-to-all-done.1.parts_ref, bf16[8,2,128,4096]{3,2,1,0:T(8,128)(2,1)} %all-gather.2.cloned.1.call-done.weight_ref), custom_call_target="tpu_custom_call" | custom-call | flops 1073741824 | bytes 12582912 | tf_op jit(solution)/shard_map/project0/pallas_call | solution.py:229
  143.5 13.2 %all-to-all-done.parts_ref = bf16[32,144,128]{2,1,0:T(8,128)(2,1)} async-done(((bf16[32,144,128]{2,1,0:T(8,128)(2,1)}), bf16[32,144,128]{2,1,0:T(8,128)(2,1)}, u32[]{:S(2)}, u32[]{:S(2)}) %all-to-all-start) | async-done | bytes 1179680 | tf_op jit(solution)/shard_map/all_to_all | solution.py:282
  156.7 6.4 %project1.1 = bf16[128,4096]{1,0:T(8,128)(2,1)} custom-call(bf16[32,144,128]{2,1,0:T(8,128)(2,1)} %all-to-all-done.parts_ref, bf16[8,2,128,4096]{3,2,1,0:T(8,128)(2,1)} %all-gather.2.cloned.1.call-done.weight_ref, f32[128,4096]{1,0:T(8,128)S(1)} %project0.1.refs_0_), custom_call_target="tpu_custom_call" | custom-call | flops 1073741824 | bytes 12582912 | tf_op jit(solution)/shard_map/project1/pallas_call | solution.py:229
  (106 shorter events, 13.1 us)
Async XLA Ops:
  6.5 131.7 %all-gather.2.cloned.1.call-start = ((), (), s32[]{:S(2)}) async-start(), calls=%async_computation.2 | async-start | bytes 18874368 | tf_op jit(solution)/shard_map/all_gather | solution.py:254
  9.5 11.7 %collective-permute-start.3 = (bf16[1024,128]{1,0:T(8,128)(2,1)}, bf16[1024,128]{1,0:T(8,128)(2,1)S(1)}, u32[]{:S(2)}, u32[]{:S(2)}) collective-permute-start(bf16[1024,128]{1,0:T(8,128)(2,1)} %get-tuple-element.54.refs_2_), channel_id=1, source_target_pairs={{0,224},{32,0},{64,32},{96,64},{128,96},{160,128},{192,160},{224,1... | collective-permute-start | bytes 786440 | tf_op jit(solution)/shard_map/ppermute | solution.py:247
  16.0 8.6 %collective-permute-start.7 = (bf16[1024,128]{1,0:T(8,128)(2,1)}, bf16[1024,128]{1,0:T(8,128)(2,1)S(1)}, u32[]{:S(2)}, u32[]{:S(2)}) collective-permute-start(bf16[1024,128]{1,0:T(8,128)(2,1)} %get-tuple-element.54.refs_2_), channel_id=1, source_target_pairs={{0,32},{32,64},{64,96},{96,128},{128,160},{160,192},{192,224},{224... | collective-permute-start | bytes 786440 | tf_op jit(solution)/shard_map/ppermute | solution.py:247
  16.0 15.4 %collective-permute-start = (bf16[1024,256]{1,0:T(8,128)(2,1)S(1)}, bf16[1024,256]{1,0:T(8,128)(2,1)S(1)}, u32[]{:S(2)}, u32[]{:S(2)}) collective-permute-start(bf16[1024,256]{1,0:T(8,128)(2,1)S(1)} %copy-done.2), channel_id=1, source_target_pairs={{0,8},{8,16},{16,24},{24,0},{1,9},{9,17},{17,25},{25,1},{2,10},{10... | collective-permute-start | bytes 1572872 | tf_op jit(solution)/shard_map/ppermute | solution.py:247
  17.2 24.7 %collective-permute-start.1 = (bf16[1024,256]{1,0:T(8,128)(2,1)S(1)}, bf16[1024,256]{1,0:T(8,128)(2,1)S(1)}, u32[]{:S(2)}, u32[]{:S(2)}) collective-permute-start(bf16[1024,256]{1,0:T(8,128)(2,1)S(1)} %copy-done.2), channel_id=1, source_target_pairs={{0,16},{8,24},{16,0},{24,8},{1,17},{9,25},{17,1},{25,9},{2,18},{10... | collective-permute-start | bytes 1572872 | tf_op jit(solution)/shard_map/ppermute | solution.py:247
  19.6 10.2 %collective-permute-start.13 = (bf16[128,1024]{1,0:T(8,128)(2,1)}, bf16[128,1024]{1,0:T(8,128)(2,1)S(1)}, u32[]{:S(2)}, u32[]{:S(2)}) collective-permute-start(bf16[128,1024]{1,0:T(8,128)(2,1)} %get-tuple-element.42.refs_10_), channel_id=1, source_target_pairs={{0,32},{32,64},{64,96},{96,128},{128,160},{160,192},{192,224},{224... | collective-permute-start | bytes 786440 | tf_op jit(solution)/shard_map/ppermute | solution.py:247
  21.2 8.6 %collective-permute-start.17 = (bf16[128,1024]{1,0:T(8,128)(2,1)}, bf16[128,1024]{1,0:T(8,128)(2,1)S(1)}, u32[]{:S(2)}, u32[]{:S(2)}) collective-permute-start(bf16[128,1024]{1,0:T(8,128)(2,1)} %get-tuple-element.42.refs_10_), channel_id=1, source_target_pairs={{0,224},{32,0},{64,32},{96,64},{128,96},{160,128},{192,160},{224,1... | collective-permute-start | bytes 786440 | tf_op jit(solution)/shard_map/ppermute | solution.py:247
  24.6 19.8 %collective-permute-start.2 = (bf16[1024,256]{1,0:T(8,128)(2,1)S(1)}, bf16[1024,256]{1,0:T(8,128)(2,1)S(1)}, u32[]{:S(2)}, u32[]{:S(2)}) collective-permute-start(bf16[1024,256]{1,0:T(8,128)(2,1)S(1)} %copy-done.2), channel_id=1, source_target_pairs={{0,24},{8,0},{16,8},{24,16},{1,25},{9,1},{17,9},{25,17},{2,26},{10... | collective-permute-start | bytes 1572872 | tf_op jit(solution)/shard_map/ppermute | solution.py:247
  29.9 14.4 %collective-permute-start.4 = (bf16[1024,128]{1,0:T(8,128)(2,1)S(1)}, bf16[1024,128]{1,0:T(8,128)(2,1)S(1)}, u32[]{:S(2)}, u32[]{:S(2)}) collective-permute-start(bf16[1024,128]{1,0:T(8,128)(2,1)S(1)} %collective-permute-done.3.refs_4_), channel_id=1, source_target_pairs={{0,224},{32,0},{64,32},{96,64},{128,96},{160,128},{192,160},{224,1... | collective-permute-start | bytes 786440 | tf_op jit(solution)/shard_map/ppermute | solution.py:247
  29.9 14.5 %collective-permute-start.8 = (bf16[1024,128]{1,0:T(8,128)(2,1)S(1)}, bf16[1024,128]{1,0:T(8,128)(2,1)S(1)}, u32[]{:S(2)}, u32[]{:S(2)}) collective-permute-start(bf16[1024,128]{1,0:T(8,128)(2,1)S(1)} %collective-permute-done.7.refs_3_), channel_id=1, source_target_pairs={{0,32},{32,64},{64,96},{96,128},{128,160},{160,192},{192,224},{224... | collective-permute-start | bytes 786440 | tf_op jit(solution)/shard_map/ppermute | solution.py:247
  31.3 14.5 %collective-permute-start.14 = (bf16[128,1024]{1,0:T(8,128)(2,1)S(1)}, bf16[128,1024]{1,0:T(8,128)(2,1)S(1)}, u32[]{:S(2)}, u32[]{:S(2)}) collective-permute-start(bf16[128,1024]{1,0:T(8,128)(2,1)S(1)} %collective-permute-done.13.refs_12_), channel_id=1, source_target_pairs={{0,32},{32,64},{64,96},{96,128},{128,160},{160,192},{192,224},{224... | collective-permute-start | bytes 786440 | tf_op jit(solution)/shard_map/ppermute | solution.py:247
  44.3 9.3 %collective-permute-start.5 = (bf16[1024,128]{1,0:T(8,128)(2,1)S(1)}, bf16[1024,128]{1,0:T(8,128)(2,1)S(1)}, u32[]{:S(2)}, u32[]{:S(2)}) collective-permute-start(bf16[1024,128]{1,0:T(8,128)(2,1)S(1)} %collective-permute-done.4.refs_6_), channel_id=1, source_target_pairs={{0,224},{32,0},{64,32},{96,64},{128,96},{160,128},{192,160},{224,1... | collective-permute-start | bytes 786440 | tf_op jit(solution)/shard_map/ppermute | solution.py:247
  44.4 12.5 %collective-permute-start.9 = (bf16[1024,128]{1,0:T(8,128)(2,1)S(1)}, bf16[1024,128]{1,0:T(8,128)(2,1)}, u32[]{:S(2)}, u32[]{:S(2)}) collective-permute-start(bf16[1024,128]{1,0:T(8,128)(2,1)S(1)} %collective-permute-done.8.refs_5_), channel_id=1, source_target_pairs={{0,32},{32,64},{64,96},{96,128},{128,160},{160,192},{192,224},{224... | collective-permute-start | bytes 786440 | tf_op jit(solution)/shard_map/ppermute | solution.py:247
  45.8 11.0 %collective-permute-start.15 = (bf16[128,1024]{1,0:T(8,128)(2,1)S(1)}, bf16[128,1024]{1,0:T(8,128)(2,1)S(1)}, u32[]{:S(2)}, u32[]{:S(2)}) collective-permute-start(bf16[128,1024]{1,0:T(8,128)(2,1)S(1)} %collective-permute-done.14.refs_14_), channel_id=1, source_target_pairs={{0,32},{32,64},{64,96},{96,128},{128,160},{160,192},{192,224},{224... | collective-permute-start | bytes 786440 | tf_op jit(solution)/shard_map/ppermute | solution.py:247
  47.9 11.2 %collective-permute-start.19 = (bf16[128,1024]{1,0:T(8,128)(2,1)S(1)}, bf16[128,1024]{1,0:T(8,128)(2,1)}, u32[]{:S(2)}, u32[]{:S(2)}) collective-permute-start(bf16[128,1024]{1,0:T(8,128)(2,1)S(1)} %collective-permute-done.18.refs_13_), channel_id=1, source_target_pairs={{0,224},{32,0},{64,32},{96,64},{128,96},{160,128},{192,160},{224,1... | collective-permute-start | bytes 786440 | tf_op jit(solution)/shard_map/ppermute | solution.py:247
  53.5 11.2 %collective-permute-start.6 = (bf16[1024,128]{1,0:T(8,128)(2,1)}, bf16[1024,128]{1,0:T(8,128)(2,1)S(1)}, u32[]{:S(2)}, u32[]{:S(2)}) collective-permute-start(bf16[1024,128]{1,0:T(8,128)(2,1)} %get-tuple-element.40.refs_4_), channel_id=1, source_target_pairs={{0,224},{32,0},{64,32},{96,64},{128,96},{160,128},{192,160},{224,1... | collective-permute-start | bytes 786440 | tf_op jit(solution)/shard_map/ppermute | solution.py:247
  57.6 9.1 %collective-permute-start.16 = (bf16[128,1024]{1,0:T(8,128)(2,1)}, bf16[128,1024]{1,0:T(8,128)(2,1)S(1)}, u32[]{:S(2)}, u32[]{:S(2)}) collective-permute-start(bf16[128,1024]{1,0:T(8,128)(2,1)} %get-tuple-element.63.refs_12_), channel_id=1, source_target_pairs={{0,32},{32,64},{64,96},{96,128},{128,160},{160,192},{192,224},{224... | collective-permute-start | bytes 786440 | tf_op jit(solution)/shard_map/ppermute | solution.py:247
  59.1 11.2 %collective-permute-start.20 = (bf16[128,1024]{1,0:T(8,128)(2,1)}, bf16[128,1024]{1,0:T(8,128)(2,1)}, u32[]{:S(2)}, u32[]{:S(2)}) collective-permute-start(bf16[128,1024]{1,0:T(8,128)(2,1)} %collective-permute-done.19.refs_15_), channel_id=1, source_target_pairs={{0,224},{32,0},{64,32},{96,64},{128,96},{160,128},{192,160},{224,1... | collective-permute-start | bytes 786440 | tf_op jit(solution)/shard_map/ppermute | solution.py:247
  63.9 18.7 %collective-permute-start.11 = (bf16[1024,128]{1,0:T(8,128)(2,1)}, bf16[1024,128]{1,0:T(8,128)(2,1)S(1)}, u32[]{:S(2)}, u32[]{:S(2)}) collective-permute-start(bf16[1024,128]{1,0:T(8,128)(2,1)} %get-tuple-element.40.refs_4_), channel_id=1, source_target_pairs={{0,32},{32,64},{64,96},{96,128},{128,160},{160,192},{192,224},{224... | collective-permute-start | bytes 786440 | tf_op jit(solution)/shard_map/ppermute | solution.py:247
  70.4 13.0 %collective-permute-start.26 = (bf16[128,1024]{1,0:T(8,128)(2,1)}, bf16[128,1024]{1,0:T(8,128)(2,1)S(1)}, u32[]{:S(2)}, u32[]{:S(2)}) collective-permute-start(bf16[128,1024]{1,0:T(8,128)(2,1)} %get-tuple-element.63.refs_12_), channel_id=1, source_target_pairs={{0,224},{32,0},{64,32},{96,64},{128,96},{160,128},{192,160},{224,1... | collective-permute-start | bytes 786440 | tf_op jit(solution)/shard_map/ppermute | solution.py:247
  73.7 9.7 %collective-permute-start.12 = (bf16[1024,128]{1,0:T(8,128)(2,1)S(1)}, bf16[1024,128]{1,0:T(8,128)(2,1)S(1)}, u32[]{:S(2)}, u32[]{:S(2)}) collective-permute-start(bf16[1024,128]{1,0:T(8,128)(2,1)S(1)} %collective-permute-done.6.refs_5_), channel_id=1, source_target_pairs={{0,224},{32,0},{64,32},{96,64},{128,96},{160,128},{192,160},{224,1... | collective-permute-start | bytes 786440 | tf_op jit(solution)/shard_map/ppermute | solution.py:247
  73.7 9.7 %collective-permute-start.23 = (bf16[128,1024]{1,0:T(8,128)(2,1)S(1)}, bf16[128,1024]{1,0:T(8,128)(2,1)S(1)}, u32[]{:S(2)}, u32[]{:S(2)}) collective-permute-start(bf16[128,1024]{1,0:T(8,128)(2,1)S(1)} %collective-permute-done.16.refs_13_), channel_id=1, source_target_pairs={{0,32},{32,64},{64,96},{96,128},{128,160},{160,192},{192,224},{224... | collective-permute-start | bytes 786440 | tf_op jit(solution)/shard_map/ppermute | solution.py:247
  82.6 12.8 %collective-permute-start.21 = (bf16[1024,128]{1,0:T(8,128)(2,1)S(1)}, bf16[1024,128]{1,0:T(8,128)(2,1)S(1)}, u32[]{:S(2)}, u32[]{:S(2)}) collective-permute-start(bf16[1024,128]{1,0:T(8,128)(2,1)S(1)} %collective-permute-done.11.refs_6_), channel_id=1, source_target_pairs={{0,32},{32,64},{64,96},{96,128},{128,160},{160,192},{192,224},{224... | collective-permute-start | bytes 786440 | tf_op jit(solution)/shard_map/ppermute | solution.py:247
  83.4 12.9 %collective-permute-start.27 = (bf16[128,1024]{1,0:T(8,128)(2,1)S(1)}, bf16[128,1024]{1,0:T(8,128)(2,1)S(1)}, u32[]{:S(2)}, u32[]{:S(2)}) collective-permute-start(bf16[128,1024]{1,0:T(8,128)(2,1)S(1)} %collective-permute-done.26.refs_14_), channel_id=1, source_target_pairs={{0,224},{32,0},{64,32},{96,64},{128,96},{160,128},{192,160},{224,1... | collective-permute-start | bytes 786440 | tf_op jit(solution)/shard_map/ppermute | solution.py:247
  87.8 13.2 %collective-permute-start.22 = (bf16[1024,128]{1,0:T(8,128)(2,1)S(1)}, bf16[1024,128]{1,0:T(8,128)(2,1)S(1)}, u32[]{:S(2)}, u32[]{:S(2)}) collective-permute-start(bf16[1024,128]{1,0:T(8,128)(2,1)S(1)} %collective-permute-done.12.refs_7_), channel_id=1, source_target_pairs={{0,224},{32,0},{64,32},{96,64},{128,96},{160,128},{192,160},{224,1... | collective-permute-start | bytes 786440 | tf_op jit(solution)/shard_map/ppermute | solution.py:247
  89.2 13.1 %collective-permute-start.28 = (bf16[128,1024]{1,0:T(8,128)(2,1)S(1)}, bf16[128,1024]{1,0:T(8,128)(2,1)S(1)}, u32[]{:S(2)}, u32[]{:S(2)}) collective-permute-start(bf16[128,1024]{1,0:T(8,128)(2,1)S(1)} %collective-permute-done.23.refs_15_), channel_id=1, source_target_pairs={{0,32},{32,64},{64,96},{96,128},{128,160},{160,192},{192,224},{224... | collective-permute-start | bytes 786440 | tf_op jit(solution)/shard_map/ppermute | solution.py:247
  95.5 19.8 %collective-permute-start.24 = (bf16[1024,128]{1,0:T(8,128)(2,1)S(1)}, bf16[1024,128]{1,0:T(8,128)(2,1)S(1)}, u32[]{:S(2)}, u32[]{:S(2)}) collective-permute-start(bf16[1024,128]{1,0:T(8,128)(2,1)S(1)} %collective-permute-done.21.refs_8_), channel_id=1, source_target_pairs={{0,32},{32,64},{64,96},{96,128},{128,160},{160,192},{192,224},{224... | collective-permute-start | bytes 786440 | tf_op jit(solution)/shard_map/ppermute | solution.py:247
  96.3 19.1 %collective-permute-start.29 = (bf16[128,1024]{1,0:T(8,128)(2,1)S(1)}, bf16[128,1024]{1,0:T(8,128)(2,1)S(1)}, u32[]{:S(2)}, u32[]{:S(2)}) collective-permute-start(bf16[128,1024]{1,0:T(8,128)(2,1)S(1)} %collective-permute-done.27.refs_16_), channel_id=1, source_target_pairs={{0,224},{32,0},{64,32},{96,64},{128,96},{160,128},{192,160},{224,1... | collective-permute-start | bytes 786440 | tf_op jit(solution)/shard_map/ppermute | solution.py:247
  101.0 14.4 %collective-permute-start.25 = (bf16[1024,128]{1,0:T(8,128)(2,1)S(1)}, bf16[1024,128]{1,0:T(8,128)(2,1)S(1)}, u32[]{:S(2)}, u32[]{:S(2)}) collective-permute-start(bf16[1024,128]{1,0:T(8,128)(2,1)S(1)} %collective-permute-done.22.refs_9_), channel_id=1, source_target_pairs={{0,224},{32,0},{64,32},{96,64},{128,96},{160,128},{192,160},{224,1... | collective-permute-start | bytes 786440 | tf_op jit(solution)/shard_map/ppermute | solution.py:247
  102.3 13.0 %collective-permute-start.30 = (bf16[128,1024]{1,0:T(8,128)(2,1)S(1)}, bf16[128,1024]{1,0:T(8,128)(2,1)S(1)}, u32[]{:S(2)}, u32[]{:S(2)}) collective-permute-start(bf16[128,1024]{1,0:T(8,128)(2,1)S(1)} %collective-permute-done.28.refs_17_), channel_id=1, source_target_pairs={{0,32},{32,64},{64,96},{96,128},{128,160},{160,192},{192,224},{224... | collective-permute-start | bytes 786440 | tf_op jit(solution)/shard_map/ppermute | solution.py:247
  103.0 30.6 %all-to-all-start.1 = ((bf16[32,144,128]{2,1,0:T(8,128)(2,1)}), bf16[32,144,128]{2,1,0:T(8,128)(2,1)S(1)}, u32[]{:S(2)}, u32[]{:S(2)}) async-start(bf16[32,144,128]{2,1,0:T(8,128)(2,1)} %attend0.3), calls=%async_computation.1 | async-start | bytes 2359296 | tf_op jit(solution)/shard_map/all_to_all | solution.py:282
  133.7 23.0 %all-to-all-start = ((bf16[32,144,128]{2,1,0:T(8,128)(2,1)}), bf16[32,144,128]{2,1,0:T(8,128)(2,1)}, u32[]{:S(2)}, u32[]{:S(2)}) async-start(bf16[32,144,128]{2,1,0:T(8,128)(2,1)} %attend1.1), calls=%async_computation | async-start | bytes 2359296 | tf_op jit(solution)/shard_map/all_to_all | solution.py:282
  (32 other events, 561.3 us)
Sparse Core Ops, SparseCore 0:
  9.2 91.7 all-gather.1
